TPU v7x, 32 devices: a whole 2x2x4 slice. The times are simulated.
32 devices in a mesh: batch: 8 (over y, x, core), row: 4 (over z).
Axes of the slice: x: 2, y: 2, z: 4, core: 2. Of those that a mesh axis runs over, the one named last changes fastest.
Arguments:
- input_field: bfloat16 [64, 128, 192, 128], P('batch', 'row'), may hold values from -6 to 6
- cotangent: bfloat16 [64, 128, 192, 128], P('batch', 'row'), may hold values from -6 to 6
- sample_scale: int32 [64], P('batch'), may hold values from 0 to 7
- scale_table: float32 [8], replicated, may hold values from 0.5 to 2
- owner_map: int32 [256], replicated, may hold values from 0 to 255, as said below
- spectral_master: float32 [256, 48, 384], P(('batch', 'row')), may hold values from -1.25 to 1.25
- spectral_momentum: float32 [256, 48, 384], P(('batch', 'row')), may hold values from -96 to 96
- pointwise_master: float32 [48, 192], replicated, may hold values from -0.3125 to 0.3125
- pointwise_momentum: float32 [48, 192], replicated, may hold values from -8192 to 8192
Outputs:
- output_field: bfloat16 [64, 128, 192, 128], P('batch', 'row')
- input_grad: bfloat16 [64, 128, 192, 128], P('batch', 'row')
- spectral_grad: float32 [256, 48, 384], P(('batch', 'row'))
- spectral_moment: float32 [256, 48, 384], P(('batch', 'row'))
- spectral_weight: float32 [256, 48, 384], P(('batch', 'row'))
- spectral_weight_low: bfloat16 [256, 48, 384], P(('batch', 'row'))
- pointwise_grad: float32 [48, 192], replicated
- pointwise_moment: float32 [48, 192], replicated
- pointwise_weight: float32 [48, 192], replicated
- pointwise_weight_low: bfloat16 [48, 192], replicated
Inputs may be any that keep to these rules, and one draw needn't show every extreme that they name: owner_map is a permutation of the 256 modes; slot t names a mode m whose column frequency l = m mod 16 satisfies l // 4 == (t // 8) mod 4.
All inputs are finite; a program needn't handle non-finite values.
Results may differ from a plain program's by a relative error of at most 0.011.
Values may be sent and summed in bfloat16 or wider, within the bound.
A program may use at most 192 MiB of HBM per device.

v0:
```python
import math

import jax
import jax.numpy as jnp
import numpy as np
from jax import lax
from jax.sharding import PartitionSpec as P

ROW_MODES = 16
COLUMN_MODES = 16


BLADE_SIGNS = np.array([[1, 1, 1, 1], [1, 1, 1, 1], [1, -1, 1, -1], [1, -1, 1, -1]], np.float32)
QUINTIC_FIRST = 3.4445
QUINTIC_SECOND = -4.775
QUINTIC_THIRD = 2.0315
SPECTRAL_RATE = 4.0
POINTWISE_RATE = 0.8
MOMENTUM_DECAY = 0.5
PRECISE = lax.Precision.HIGHEST


def angles_of(first, second, grid_size):
    return 2.0 * math.pi / grid_size * (first * second % grid_size).astype(jnp.float32)


def row_frequencies(grid_size, mode_count):
    indices = jnp.arange(mode_count, dtype=jnp.int32)
    return jnp.where(indices < mode_count // 2, indices, grid_size - mode_count + indices)


def column_table(grid_size, mode_count):
    position = jnp.arange(grid_size, dtype=jnp.int32)[:, None]
    frequency = jnp.arange(mode_count, dtype=jnp.int32)[None, :]
    angles = angles_of(position, frequency, grid_size)
    return jnp.concatenate([jnp.cos(angles), -jnp.sin(angles)], axis=1).astype(jnp.bfloat16)


def row_table(grid_size, mode_count):
    frequency = row_frequencies(grid_size, mode_count)[:, None]
    position = jnp.arange(grid_size, dtype=jnp.int32)[None, :]
    angles = angles_of(frequency, position, grid_size)
    cosine, sines = (jnp.cos(angles), jnp.sin(angles))
    upper_half = jnp.stack([cosine, sines], axis=-1)
    bottom = jnp.stack([-sines, cosine], axis=-1)
    return (
        jnp.stack([upper_half, bottom], axis=0)
        .reshape(2 * mode_count, 2 * grid_size)
        .astype(jnp.bfloat16)
    )


def inverse_row_table(grid_size, mode_count):
    position = jnp.arange(grid_size, dtype=jnp.int32)[:, None]
    frequency = row_frequencies(grid_size, mode_count)[None, :]
    angles = angles_of(position, frequency, grid_size)
    cosine, sines = (jnp.cos(angles), jnp.sin(angles))
    real_rows = jnp.stack([cosine, -sines], axis=1)
    imaginary_rows = jnp.stack([sines, cosine], axis=1)
    return (
        jnp.stack([real_rows, imaginary_rows], axis=1)
        .reshape(2 * grid_size, 2 * mode_count)
        .astype(jnp.bfloat16)
    )


def inverse_column_table(grid_size, mode_count):
    frequency = jnp.arange(mode_count, dtype=jnp.int32)[:, None]
    position = jnp.arange(grid_size, dtype=jnp.int32)[None, :]
    angles = angles_of(frequency, position, grid_size)
    weight = jnp.where(frequency == 0, 1.0, 2.0) / (grid_size * grid_size)
    return jnp.concatenate([weight * jnp.cos(angles), -weight * jnp.sin(angles)], axis=0).astype(
        jnp.bfloat16
    )


def expand(blade_parts):
    channels = blade_parts.shape[-1]
    source = np.array([[k ^ a for a in range(4)] for k in range(4)], np.int32)
    sign_table = np.array([[BLADE_SIGNS[a, k ^ a] for a in range(4)] for k in range(4)], np.float32)
    picked = blade_parts[..., source, :] * jnp.asarray(sign_table, blade_parts.dtype)[:, :, None]
    real_part = picked[..., 0, :, :, :]
    imaginary = picked[..., 1, :, :, :]
    upper_half = jnp.stack([real_part, -imaginary], axis=-3)
    bottom = jnp.stack([imaginary, real_part], axis=-3)
    stacked = jnp.stack([upper_half, bottom], axis=-4)
    return stacked.reshape(stacked.shape[:-5] + (8, 8 * channels))


def point_kernel(point_weight):
    channels = point_weight.shape[0]
    source = np.array([[k ^ b for k in range(4)] for b in range(4)], np.int32)
    sign_table = np.array([[BLADE_SIGNS[k ^ b, b] for k in range(4)] for b in range(4)], np.float32)
    blades = point_weight.reshape(channels, 4, channels)
    picked = blades[:, source, :] * jnp.asarray(sign_table, point_weight.dtype)[None, :, :, None]
    return picked.transpose(1, 3, 2, 0).reshape(4 * channels, 4 * channels)


def orthogonalize(matrices):
    norm_size = jnp.sqrt(jnp.sum(matrices * matrices, axis=(-2, -1), keepdims=True))
    current = matrices / (norm_size + 1e-07)
    for repeat in range(5):
        gram_matrix = jnp.einsum("...ij,...kj->...ik", current, current, precision=PRECISE)
        polynomial = QUINTIC_SECOND * gram_matrix + QUINTIC_THIRD * jnp.einsum(
            "...ij,...jk->...ik", gram_matrix, gram_matrix, precision=PRECISE
        )
        current = QUINTIC_FIRST * current + jnp.einsum(
            "...ij,...jk->...ik", polynomial, current, precision=PRECISE
        )
    return current


def per_device(
    input_field,
    cotangent,
    sample_scale,
    scale_table,
    owner_map,
    spectral_master,
    spectral_momentum,
    pointwise_master,
    pointwise_momentum,
):
    samples_here, rows_here, blade_width, grid_size = input_field.shape
    channels = blade_width // 4
    row_count = lax.axis_size("row")
    batch_count = lax.axis_size("batch")
    row_index = lax.axis_index("row")
    local_columns = COLUMN_MODES // row_count
    local_modes = ROW_MODES * local_columns
    slots_here = spectral_master.shape[0]
    float_type = jnp.float32
    low_type = jnp.bfloat16
    column_fwd = column_table(grid_size, COLUMN_MODES)
    row_fwd = row_table(grid_size, ROW_MODES)
    row_inv = inverse_row_table(grid_size, ROW_MODES)
    column_inv = inverse_column_table(grid_size, COLUMN_MODES)
    group_ids = jnp.arange(batch_count * slots_here, dtype=jnp.int32)
    group_slot = (
        group_ids // slots_here * row_count + row_index
    ) * slots_here + group_ids % slots_here
    group_mode = jnp.take(owner_map, group_slot)
    group_local = group_mode // COLUMN_MODES * local_columns + group_mode % local_columns
    local_ids = jnp.arange(local_modes, dtype=jnp.int32)
    matches = group_local[None, :] == local_ids[:, None]
    slot_of = jnp.sum(jnp.where(matches, group_ids[None, :], 0), axis=1)
    gathered = lax.all_gather(spectral_master.astype(low_type), "batch", axis=0, tiled=True)
    local_weights = jnp.take(gathered, slot_of, axis=0)
    columns = jnp.einsum(
        "shkw,wm->shmk", input_field, column_fwd, preferred_element_type=float_type
    ).astype(low_type)
    columns = columns.reshape(samples_here, rows_here, 2, COLUMN_MODES, blade_width)
    by_rows = lax.all_to_all(columns, "row", split_axis=3, concat_axis=1, tiled=True)
    by_rows = by_rows.reshape(samples_here, 2 * grid_size, local_columns, blade_width)
    spectra = jnp.einsum(
        "xy,syqk->sxqk", row_fwd, by_rows, preferred_element_type=float_type
    ).astype(low_type)
    blade_parts = spectra.reshape(samples_here, 2, ROW_MODES, local_columns, 4, channels).transpose(
        0, 2, 3, 1, 4, 5
    )
    blade_parts = blade_parts.reshape(samples_here, local_modes, 2, 4, channels)
    spread = expand(blade_parts)
    product = jnp.einsum(
        "smyz,moz->smyo", spread, local_weights, preferred_element_type=float_type
    ).astype(low_type)
    product_rows = product.reshape(
        samples_here, ROW_MODES, local_columns, 4, 2, channels
    ).transpose(0, 4, 1, 2, 3, 5)
    product_rows = product_rows.reshape(samples_here, 2 * ROW_MODES, local_columns, blade_width)
    rows_back = jnp.einsum(
        "yx,sxqk->syqk", row_inv, product_rows, preferred_element_type=float_type
    ).astype(low_type)
    rows_back = rows_back.reshape(samples_here, grid_size, 2, local_columns, blade_width)
    mixed_cols = lax.all_to_all(rows_back, "row", split_axis=1, concat_axis=3, tiled=True)
    mixed_cols = mixed_cols.reshape(samples_here, rows_here, 2 * COLUMN_MODES, blade_width)
    spectral = jnp.einsum(
        "shmk,mw->shkw", mixed_cols, column_inv, preferred_element_type=float_type
    )
    kernel = point_kernel(pointwise_master.astype(low_type))
    pointwise_part = jnp.einsum(
        "shkw,kj->shjw", input_field, kernel, preferred_element_type=float_type
    )
    factors = jnp.take(scale_table, sample_scale)[:, None, None, None]
    branch = spectral + pointwise_part
    activated, gelu_back = jax.vjp(jax.nn.gelu, factors * branch)
    output_field = (input_field.astype(float_type) + activated).astype(low_type)
    cot_values = cotangent.astype(float_type)
    grad_before = gelu_back(cot_values)[0]
    grad_branch = (factors * grad_before).astype(low_type)
    grad_point_input = jnp.einsum(
        "shjw,kj->shkw", grad_branch, kernel, preferred_element_type=float_type
    )
    grad_kernel = jnp.einsum(
        "shkw,shjw->kj", input_field, grad_branch, preferred_element_type=float_type
    )
    unused_kernel, kernel_back = jax.vjp(point_kernel, pointwise_master)
    local_point_grad = kernel_back(grad_kernel)[0]
    pointwise_grad = lax.psum(local_point_grad, ("batch", "row"))
    grad_mixed = jnp.einsum(
        "shkw,mw->shmk", grad_branch, column_inv, preferred_element_type=float_type
    ).astype(low_type)
    grad_mixed = grad_mixed.reshape(samples_here, rows_here, 2, COLUMN_MODES, blade_width)
    grad_rows = lax.all_to_all(grad_mixed, "row", split_axis=3, concat_axis=1, tiled=True)
    grad_rows = grad_rows.reshape(samples_here, 2 * grid_size, local_columns, blade_width)
    grad_product = jnp.einsum(
        "yx,syqk->sxqk", row_inv, grad_rows, preferred_element_type=float_type
    ).astype(low_type)
    grad_product = grad_product.reshape(
        samples_here, 2, ROW_MODES, local_columns, 4, channels
    ).transpose(0, 2, 3, 4, 1, 5)
    grad_product = grad_product.reshape(samples_here, local_modes, 8, channels)
    grad_spread = jnp.einsum(
        "smyo,moz->smyz", grad_product, local_weights, preferred_element_type=float_type
    )
    unused_spread, spread_back = jax.vjp(expand, blade_parts.astype(float_type))
    grad_parts = spread_back(grad_spread)[0]
    grad_spectra = grad_parts.reshape(
        samples_here, ROW_MODES, local_columns, 2, 4, channels
    ).transpose(0, 3, 1, 2, 4, 5)
    grad_spectra = grad_spectra.reshape(
        samples_here, 2 * ROW_MODES, local_columns, blade_width
    ).astype(low_type)
    grad_by_rows = jnp.einsum(
        "xy,sxqk->syqk", row_fwd, grad_spectra, preferred_element_type=float_type
    ).astype(low_type)
    grad_by_rows = grad_by_rows.reshape(samples_here, grid_size, 2, local_columns, blade_width)
    grad_columns = lax.all_to_all(grad_by_rows, "row", split_axis=1, concat_axis=3, tiled=True)
    grad_columns = grad_columns.reshape(samples_here, rows_here, 2 * COLUMN_MODES, blade_width)
    grad_spectral_input = jnp.einsum(
        "shmk,wm->shkw", grad_columns, column_fwd, preferred_element_type=float_type
    )
    input_grad = (cot_values + grad_point_input + grad_spectral_input).astype(low_type)
    local_grad = jnp.einsum(
        "smyo,smyz->moz", grad_product, spread, preferred_element_type=float_type
    )
    ordered = jnp.take(local_grad, group_local, axis=0)
    spectral_grad = lax.psum_scatter(ordered, "batch", scatter_dimension=0, tiled=True)
    spectral_moment = MOMENTUM_DECAY * spectral_momentum + spectral_grad
    spectral_weight = spectral_master - SPECTRAL_RATE * orthogonalize(spectral_moment)
    pointwise_moment = MOMENTUM_DECAY * pointwise_momentum + pointwise_grad
    pointwise_weight = pointwise_master - POINTWISE_RATE * orthogonalize(pointwise_moment)
    return (
        output_field,
        input_grad,
        spectral_grad,
        spectral_moment,
        spectral_weight,
        spectral_weight.astype(low_type),
        pointwise_grad,
        pointwise_moment,
        pointwise_weight,
        pointwise_weight.astype(low_type),
    )


def solution(mesh):
    return jax.shard_map(
        per_device,
        mesh=mesh,
        in_specs=(
            P("batch", "row", None, None),
            P("batch", "row", None, None),
            P("batch"),
            P(),
            P(),
            P(("batch", "row"), None, None),
            P(("batch", "row"), None, None),
            P(),
            P(),
        ),
        out_specs=(
            P("batch", "row", None, None),
            P("batch", "row", None, None),
            P(("batch", "row"), None, None),
            P(("batch", "row"), None, None),
            P(("batch", "row"), None, None),
            P(("batch", "row"), None, None),
            P(),
            P(),
            P(),
            P(),
        ),
        check_vma=False,
    )
```

profile of v0, /device:TPU:0, one launch (start us, length us, event | category | flops | bytes accessed | tf_op | source)
XLA Modules:
  0.0 768.3 jit_solution(15436807177350407668)
XLA Ops:
  7.3 12.6 %convolution_convert_fusion.1 = bf16[32,8,32,192]{3,0,2,1:T(8,128)(2,1)S(1)} fusion(bf16[8,32,192,128]{3,2,1,0:T(8,128)(2,1)} %param.21, bf16[128,16]{0,1:T(8,128)(2,1)S(1)} %get-tuple-element.38, bf16[128,16]{0,1:T(8,128)(2,1)S(1)} %get-tuple-element.39), kind=kOutput, calls=%fused_computation.60 | convolution fusion | flops 404242432 | bytes 15736832 | tf_op jit(solution)/shard_map/shkw,wm->shmk/dot_general | solution.py:149
  24.4 6.5 all-to-all-start
  34.2 30.4 %all-gather.2.cloned.1.call-done = bf16[64,48,384]{2,1,0:T(8,128)(2,1)} async-done(((bf16[8,48,384]{2,1,0:T(8,128)(2,1)}), bf16[64,48,384]{2,1,0:T(8,128)(2,1)}) %all-gather.2.cloned.1.call-update) | async-done | bytes 2359312 | tf_op jit(solution)/shard_map/all_gather | solution.py:147
  68.6 55.6 %all-to-all-done = bf16[8,32,2,16,192]{4,1,2,0,3:T(8,128)(2,1)} async-done(((bf16[8,32,2,16,192]{4,1,2,0,3:T(8,128)(2,1)}), bf16[8,32,2,16,192]{4,1,2,0,3:T(8,128)(2,1)}, u32[]{:S(2)}, u32[]{:S(2)}) %all-to-all-start) | async-done | bytes 3145760 | tf_op jit(solution)/shard_map/all_to_all | solution.py:153
  139.5 7.7 copy.168
  153.6 6.3 maximum_bitcast_fusion
  159.9 7.7 pad_maximum_fusion
  167.5 12.3 %reshape.724 = bf16[8,64,8,384]{3,2,1,0:T(8,128)(2,1)S(1)} reshape(bf16[8,64,4,2,2,4,48]{6,5,4,3,2,1,0:T(4,128)(2,1)} %pad_maximum_fusion) | data formatting | bytes 6291456 | tf_op jit(solution)/shard_map/reshape | solution.py:87
  190.1 5.5 copy.174
  202.6 90.7 %all-to-all-done.1 = bf16[8,128,2,4,192]{4,0,3,2,1:T(8,128)(2,1)} async-done(((bf16[8,128,2,4,192]{4,0,3,2,1:T(8,128)(2,1)}), bf16[8,128,2,4,192]{4,0,3,2,1:T(8,128)(2,1)}, u32[]{:S(2)}, u32[]{:S(2)}) %all-to-all-start.1) | async-done | bytes 3145760 | tf_op jit(solution)/shard_map/all_to_all | solution.py:174
  293.3 6.6 copy.253
  299.9 7.5 reshape.728
  307.4 11.9 %fusion.103 = f32[8,32,192,128]{3,2,1,0:T(8,128)} fusion(bf16[8,32,32,192]{3,2,1,0:T(8,128)(2,1)} %reshape.728, bf16[16,128]{1,0:T(8,128)(2,1)S(1)} %get-tuple-element.40, bf16[16,128]{1,0:T(8,128)(2,1)S(1)} %get-tuple-element.41), kind=kOutput, calls=%fused_computation.179 | convolution fusion | flops 402669568 | bytes 28319744 | tf_op jit(solution)/shard_map/shmk,mw->shkw/dot_general | solution.py:176
  319.3 37.3 %fusion.7 = (bf16[8,32,192,128]{3,2,1,0:T(8,128)(2,1)}, bf16[8,32,192,128]{3,2,1,0:T(8,128)(2,1)}) fusion(bf16[8,32,192,128]{3,2,1,0:T(8,128)(2,1)} %param.22, f32[8]{0:T(128)S(1)} %and_select_fusion.10, bf16[8,32,192,128]{3,2,1,0:T(8,128)(2,1)} %param.21, f32[8,32,192,128]{3,2,1,0:T(8,128)} %fusion.103, bf16[192,192]{1,0:T(8,128)(2,1)S(1)} %reshape.730), kind=kOutput, calls=%fused_computation.20 | convolution fusion | flops 2592079872 | bytes 75571232 | tf_op jit(solution)/shard_map/shkw,kj->shjw/dot_general | solution.py:180
  356.6 12.6 %convolution_convert_fusion = bf16[32,8,32,192]{3,0,2,1:T(8,128)(2,1)S(1)} fusion(bf16[8,32,192,128]{3,2,1,0:T(8,128)(2,1)} %get-tuple-element.16, bf16[16,128]{1,0:T(8,128)(2,1)S(1)} %get-tuple-element.40, bf16[16,128]{1,0:T(8,128)(2,1)S(1)} %get-tuple-element.41), kind=kOutput, calls=%fused_computation.59 | convolution fusion | flops 404242432 | bytes 15736832 | tf_op jit(solution)/shard_map/shkw,mw->shmk/dot_general | solution.py:199
  378.8 10.0 %fusion.58 = f32[192,192]{0,1:T(8,128)S(1)} fusion(bf16[8,32,192,128]{3,2,1,0:T(8,128)(2,1)} %param.21, bf16[8,32,192,128]{3,2,1,0:T(8,128)(2,1)} %get-tuple-element.16), kind=kOutput, calls=%fused_computation.90 | convolution fusion | flops 2415919104 | bytes 25313280 | tf_op jit(solution)/shard_map/shkw,shjw->kj/dot_general | solution.py:193
  390.9 100.8 %psum.7 = f32[48,192]{1,0:T(8,128)S(1)} all-reduce(f32[48,192]{1,0:T(8,128)S(1)} %reshape.739), channel_id=1, replica_groups=mesh['batch'=8,'row'=4] {'batch','row'}, use_global_device_ids=true, to_apply=%region_5.6 | all-reduce | flops 9216 | bytes 73728 | tf_op jit(solution)/shard_map/psum | solution.py:198
  496.3 5.4 fusion.47
  514.9 17.5 %reshape.735 = f32[8,64,4,2,2,4,48]{6,5,4,3,2,1,0:T(4,128)} reshape(f32[8,64,8,384]{3,2,1,0:T(8,128)} %copy.185) | data formatting | bytes 12582912 | tf_op jit(solution)/shard_map/transpose(jvp())/reshape | solution.py:87
  532.4 13.0 %fusion.131 = (f32[8,64,4,1,2,4,48]{6,5,4,3,2,1,0:T(4,128)}, f32[8,64,4,2,4,48]{5,4,3,2,1,0:T(4,128)}) fusion(f32[8,64,4,2,2,4,48]{6,5,4,3,2,1,0:T(4,128)} %reshape.735), kind=kLoop, calls=%fused_computation.248 | loop fusion | bytes 12582912 | tf_op jit(solution)/shard_map/transpose(jvp())/unstack | solution.py:86
  545.4 8.8 %copy.251 = f32[8,64,4,1,2,4,48]{6,5,2,1,0,4,3:T(4,128)} copy(f32[8,64,4,1,2,4,48]{6,5,4,3,2,1,0:T(4,128)} %get-tuple-element.18) | data formatting | bytes 6291456
  554.2 7.1 fusion.20
  566.5 5.4 gather_fusion.5
  577.5 9.6 %add_multiply_fusion = f32[8,64,2,4,4,48]{5,4,3,1,0,2:T(4,128)} fusion(f32[8,64,1,4,4,48]{5,4,3,1,0,2:T(4,128)} %fusion.17, f32[8,64,1,4,4,48]{5,4,3,1,0,2:T(4,128)} %fusion.20, f32[4,4]{1,0:T(4,128)S(1)} %copy-done.23), kind=kLoop, calls=%fused_computation.35 | loop fusion | flops 1572864 | bytes 6291520 | tf_op jit(solution)/shard_map/transpose(jvp())/mul | solution.py:81
  587.1 8.8 %copy.189 = f32[16,8,64,2,48]{2,4,3,1,0:T(8,128)} copy(f32[16,8,64,2,48]{4,0,2,1,3:T(8,128)} %bitcast.252) | data formatting | bytes 6291456 | tf_op jit(solution)/shard_map/transpose(jvp())/mul | solution.py:81
  596.0 10.3 %scatter_fusion = f32[8,64,2,4,48]{1,4,3,2,0:T(8,128)S(1)} fusion(f32[8,64,2,4,48]{1,4,3,2,0:T(8,128)S(1)} %broadcast_in_dim.99, s32[16]{0:T(128)S(1)} %copy-done.18, f32[16,8,64,2,48]{2,4,3,1,0:T(8,128)} %copy.189), kind=kCustom, calls=%fused_computation.6 | custom fusion | flops 786432 | bytes 9437248 | tf_op jit(solution)/shard_map/transpose(jvp())/scatter-add | solution.py:81
  612.2 5.7 copy.193
  628.0 16.5 %fusion.71 = f32[192,8,32,128]{3,0,2,1:T(8,128)} fusion(bf16[8,32,192,128]{3,2,1,0:T(8,128)(2,1)} %get-tuple-element.16, bf16[192,192,1,1]{1,0,2,3:T(8,128)(2,1)S(1)} %reshape.815), kind=kOutput, calls=%fused_computation.114 | convolution fusion | flops 2415919104 | bytes 37822464 | tf_op jit(solution)/shard_map/shjw,kj->shkw/dot_general | solution.py:190
  644.5 70.9 %all-to-all-done.3 = bf16[8,128,2,4,192]{4,0,3,2,1:T(8,128)(2,1)} async-done(((bf16[8,128,2,4,192]{4,0,3,2,1:T(8,128)(2,1)}), bf16[8,128,2,4,192]{4,0,3,2,1:T(8,128)(2,1)}, u32[]{:S(2)}, u32[]{:S(2)}) %all-to-all-start.3) | async-done | bytes 3145760 | tf_op jit(solution)/shard_map/all_to_all | solution.py:227
  715.4 6.6 copy.252
  722.0 7.6 reshape.737
  729.6 19.9 %fusion.12 = bf16[8,32,192,128]{3,2,1,0:T(8,128)(2,1)} fusion(bf16[8,32,192,128]{3,2,1,0:T(8,128)(2,1)} %param.22, f32[192,8,32,128]{3,0,2,1:T(8,128)} %fusion.71, bf16[8,32,32,192]{3,2,1,0:T(8,128)(2,1)} %reshape.737, bf16[128,16]{0,1:T(8,128)(2,1)S(1)} %copy-done.20, bf16[128,16]{0,1:T(8,128)(2,1)S(1)} %copy-done.22), kind=kOutput, calls=%fused_computation.25 | convolution fusion | flops 427835392 | bytes 53485568 | tf_op jit(solution)/shard_map/shmk,wm->shkw/dot_general | solution.py:229
  (176 shorter events, 117.1 us)
Async XLA Ops:
  7.2 25.5 %copy-start = (s32[256]{0:T(256)S(1)}, s32[256]{0:T(256)}, u32[]{:S(2)}) copy-start(s32[256]{0:T(256)} %param.25) | copy-start | bytes 3076
  7.3 12.6 %copy-start.19 = (bf16[128,16]{0,1:T(8,128)(2,1)}, bf16[128,16]{0,1:T(8,128)(2,1)S(1)}, u32[]{:S(2)}) copy-start(bf16[128,16]{0,1:T(8,128)(2,1)S(1)} %get-tuple-element.38) | copy-start | bytes 12292
  7.3 12.7 %copy-start.21 = (bf16[128,16]{0,1:T(8,128)(2,1)}, bf16[128,16]{0,1:T(8,128)(2,1)S(1)}, u32[]{:S(2)}) copy-start(bf16[128,16]{0,1:T(8,128)(2,1)S(1)} %get-tuple-element.39) | copy-start | bytes 12292
  24.4 6.7 copy-start.7
  24.4 9.1 %copy-start.18 = (s32[16]{0:T(128)S(1)}, s32[16]{0:T(128)}, u32[]{:S(2)}) copy-start(s32[16]{0:T(128)} %constant.235) | copy-start | bytes 196
  24.4 99.9 %all-to-all-start = ((bf16[8,32,2,16,192]{4,1,2,0,3:T(8,128)(2,1)}), bf16[8,32,2,16,192]{4,1,2,0,3:T(8,128)(2,1)}, u32[]{:S(2)}, u32[]{:S(2)}) async-start(bf16[8,32,2,16,192]{4,1,2,0,3:T(8,128)(2,1)} %copy.160), calls=%async_computation | async-start | bytes 8388608 | tf_op jit(solution)/shard_map/all_to_all | solution.py:153
  30.8 33.8 %all-gather.2.cloned.1.call-start = ((), (), s32[]{:S(2)}) async-start(), calls=%async_computation.5 | async-start | bytes 2654208 | tf_op jit(solution)/shard_map/all_gather | solution.py:147
  32.3 96.6 %copy-start.11 = (bf16[32,256]{0,1:T(8,128)(2,1)}, bf16[32,256]{0,1:T(8,128)(2,1)S(1)}, u32[]{:S(2)}) copy-start(bf16[32,256]{0,1:T(8,128)(2,1)S(1)} %convert_element_type.175) | copy-start | bytes 49156
  139.5 7.7 copy-start.27
  179.8 5.5 copy-start.4
  195.6 5.0 copy-start.13
  195.6 5.7 copy-start.26
  195.6 6.2 copy-start.28
  195.6 6.2 copy-start.2
  195.6 97.6 %all-to-all-start.1 = ((bf16[8,128,2,4,192]{4,0,3,2,1:T(8,128)(2,1)}), bf16[8,128,2,4,192]{4,0,3,2,1:T(8,128)(2,1)}, u32[]{:S(2)}, u32[]{:S(2)}) async-start(bf16[8,128,2,4,192]{4,0,3,2,1:T(8,128)(2,1)} %bitcast.255), calls=%async_computation.1 | async-start | bytes 8388608 | tf_op jit(solution)/shard_map/all_to_all | solution.py:174
  373.7 118.0 %all-to-all-start.2 = ((bf16[8,32,2,16,192]{4,1,2,0,3:T(8,128)(2,1)}), bf16[8,32,2,16,192]{4,1,2,0,3:T(8,128)(2,1)}, u32[]{:S(2)}, u32[]{:S(2)}) async-start(bf16[8,32,2,16,192]{4,1,2,0,3:T(8,128)(2,1)} %copy.179), calls=%async_computation.2 | async-start | bytes 8388608 | tf_op jit(solution)/shard_map/all_to_all | solution.py:203
  378.5 371.0 %reduce-scatter.2.cloned.1.call-start = ((), (), s32[]{:S(2)}) async-start(), calls=%async_computation.6 | async-start | bytes 5308416 | tf_op jit(solution)/shard_map/reduce_scatter | solution.py:237
  378.8 10.3 %copy-start.24 = (f32[4,4]{0,1:T(4,128)S(1)}, f32[4,4]{0,1:T(4,128)}, u32[]{:S(2)}) copy-start(f32[4,4]{0,1:T(4,128)} %constant.226.clone) | copy-start | bytes 196
  491.7 131.6 %copy-start.15 = (f32[48,192]{1,0:T(8,128)}, f32[48,192]{1,0:T(8,128)S(1)}, u32[]{:S(2)}) copy-start(f32[48,192]{1,0:T(8,128)S(1)} %psum.7) | copy-start | bytes 110596
  496.3 11.4 %copy-start.5 = (bf16[8,64,8,384]{3,2,1,0:T(8,128)(2,1)S(1)}, bf16[8,64,8,384]{3,2,1,0:T(8,128)(2,1)}, u32[]{:S(2)}) copy-start(bf16[8,64,8,384]{3,2,1,0:T(8,128)(2,1)} %copy-done.4) | copy-start | bytes 9437188
  554.2 7.1 copy-start.3
  566.5 5.4 copy-start.25
  617.9 5.4 copy-start.16
  617.9 9.2 %copy-start.14 = (f32[48,192]{1,0:T(8,128)S(1)}, f32[48,192]{1,0:T(8,128)}, u32[]{:S(2)}) copy-start(f32[48,192]{1,0:T(8,128)} %param.28) | copy-start | bytes 110596
  617.9 97.4 %all-to-all-start.3 = ((bf16[8,128,2,4,192]{4,0,3,2,1:T(8,128)(2,1)}), bf16[8,128,2,4,192]{4,0,3,2,1:T(8,128)(2,1)}, u32[]{:S(2)}, u32[]{:S(2)}) async-start(bf16[8,128,2,4,192]{4,0,3,2,1:T(8,128)(2,1)} %bitcast.254), calls=%async_computation.3 | async-start | bytes 8388608 | tf_op jit(solution)/shard_map/all_to_all | solution.py:227
  623.9 20.5 %copy-start.17 = (f32[48,192]{1,0:T(8,128)}, f32[48,192]{1,0:T(8,128)S(1)}, u32[]{:S(2)}) copy-start(f32[48,192]{1,0:T(8,128)S(1)} %get-tuple-element.11) | copy-start | bytes 110596
  722.0 7.6 copy-start.20
  722.0 7.6 copy-start.22
  729.6 19.9 %copy-start.9 = (f32[8,48,384]{2,1,0:T(8,128)S(1)}, f32[8,48,384]{2,1,0:T(8,128)}, u32[]{:S(2)}) copy-start(f32[8,48,384]{2,1,0:T(8,128)} %param.27) | copy-start | bytes 1769476
  750.8 3.8 copy-start.10
  753.9 5.4 copy-start.8
  754.6 6.4 copy-start.1
  (3 other events, 7.6 us)
Sparse Core Ops, SparseCore 0:
  34.1 30.4 all-gather.1
  577.0 53.6 reduce-scatter.1
where the time goes:
time: 775 us; the launch traced here: 768 us
  waiting for transfers between devices  248 us (32%)
  local copies, waits for them, and re-layouts  164 us (21%)
  matrix products  156 us (20%)
  blocking collectives  101 us (13%)
  other arithmetic  61.6 us (8%)
  starting transfers between devices  21.9 us (3%)
  between operations  16.2 us (2%)
    psum x1, blocking collectives, per_device(): pointwise_grad = lax.psum(local_point_grad, ('batch', 'row'))  101 us
    all_to_all x1, waiting for transfers between devices, per_device(): lax.all_to_all(rows_back, 'row', split_axis=1, concat_axis=3, tiled=True)  90.7 us
    all_to_all x1, waiting for transfers between devices, per_device(): lax.all_to_all(grad_by_rows, 'row', split_axis=1, concat_axis=3, tiled=True)  70.9 us
    all_to_all x1, waiting for transfers between devices, per_device(): lax.all_to_all(columns, 'row', split_axis=3, concat_axis=1, tiled=True)  55.6 us
    dot_general x1, matrix products, per_device(): jnp.einsum('shkw,kj->shjw', input_field, kernel, preferred_element_type=f...  37.3 us
    all_gather x1, waiting for transfers between devices, per_device(): lax.all_gather(spectral_master.astype(low_type), 'batch', axis=0, tiled=T...  30.4 us
    reshape x2, local copies, waits for them, and re-layouts, expand(): return stacked.reshape(stacked.shape[:-5] + (8, 8 * channels))  29.8 us
    dot_general x1, matrix products, per_device(): jnp.einsum('shmk,wm->shkw', grad_columns, column_fwd, preferred_element_t...  19.9 us
  transfers between devices with their start and end apart: 6, of which 4 were waited for; matrix products, arithmetic and copies ran while one was open for 15% of the time, Pallas kernels for 0%

commit v1 on v0

v1 whole, which is shorter than its diff:
```python
import functools
import math

import jax
import jax.numpy as jnp
import ml_dtypes
import numpy as np
from jax import lax
from jax.experimental import pallas as pl
from jax.experimental.pallas import tpu as pltpu
from jax.sharding import PartitionSpec as P

ROW_MODES = 16
COLUMN_MODES = 16

BLADE_SIGNS = np.array([[1, 1, 1, 1], [1, 1, 1, 1], [1, -1, 1, -1], [1, -1, 1, -1]], np.float32)
QUINTIC_FIRST = 3.4445
QUINTIC_SECOND = -4.775
QUINTIC_THIRD = 2.0315
SPECTRAL_RATE = 4.0
POINTWISE_RATE = 0.8
MOMENTUM_DECAY = 0.5
PRECISE = lax.Precision.HIGHEST
MESH = pl.DeviceIdType.MESH
F32 = jnp.float32
BF16 = jnp.bfloat16
GELU_A = math.sqrt(2.0 / math.pi)
GELU_B = GELU_A * 0.044715


def column_block(grid_size):
    angles = 2.0 * np.pi / grid_size * (np.arange(COLUMN_MODES)[:, None] * np.arange(grid_size)[None] % grid_size)
    table = np.concatenate([np.cos(angles), -np.sin(angles)], 0)
    return np.kron(np.eye(2), table).astype(ml_dtypes.bfloat16)


def row_blocks(grid_size, row_count):
    rows = grid_size // row_count
    local = COLUMN_MODES // row_count
    r = np.arange(ROW_MODES)
    frequency = np.where(r < ROW_MODES // 2, r, grid_size - ROW_MODES + r)
    angles = 2.0 * np.pi / grid_size * (frequency[:, None] * np.arange(grid_size)[None] % grid_size)
    cosine, sine = np.cos(angles), np.sin(angles)
    table = np.stack([np.stack([cosine, sine], -1), np.stack([-sine, cosine], -1)], 0)
    table = table.reshape(2, ROW_MODES, row_count, rows, 2)
    same = np.eye(COLUMN_MODES).reshape(row_count, local, COLUMN_MODES)
    full = np.einsum("qrzhp,cdl->zqcrdhpl", table, same)
    return full.reshape(
        row_count, 2 * ROW_MODES * COLUMN_MODES, rows * 2 * COLUMN_MODES
    ).astype(ml_dtypes.bfloat16)


def product_signs(channels):
    signs = np.zeros((2, 4, 2, 4, 2, 4), np.float32)
    for q in range(2):
        for p in range(2):
            pw = p ^ q
            part = -1.0 if (q == 0 and p == 1) else 1.0
            for k in range(4):
                for b in range(4):
                    signs[q, k, pw, k ^ b, p, b] = part * BLADE_SIGNS[k ^ b, b]
    full = np.einsum("qkwapb,ij->qkwaipbj", signs, np.eye(channels, dtype=np.float32))
    return full.reshape(8, 8 * channels, 8 * channels).astype(ml_dtypes.bfloat16)


def dot(a, b):
    return lax.dot_general(a, b, (((1,), (0,)), ((), ())), preferred_element_type=F32)


def dot_nt(a, b):
    return lax.dot_general(a, b, (((1,), (1,)), ((), ())), preferred_element_type=F32)


def layer_kernel(
    sizes,
    x_hbm, ct_hbm, factor, rk_hbm, pi_hbm, cblk_ref, eye_ref, perm_ref, master_ref, point_ref,
    out_hbm, gb_hbm, dw_ref, pg_ref, kk_ref, gb2,
    xb, cb, rk, pi, bigw, cols, res, l2, kt1, ktb, acc, gk_ref, pa, pz,
    pb1, rb1, gb1, pb2, rb2,
    xs, xr, ps, pr, gs, gr, hs, hr,
    x_sem, g_sem, ld_sem, ci_sem, co_sem, pa_s, pa_r, pz_s, pz_r,
    rs1_s, rs1_r, rs2_s, rs2_r, ag1_s, ag1_r, ag2_s, ag2_r, a2a_s, a2a_r,
):
    nb, nz, S, H, K, W, slots, M = sizes
    wide = 2 * K
    channels = K // 4
    pairs = H // 2
    me = lax.axis_index("batch")
    z = lax.axis_index("row")
    last = nz - 1

    loads = [pltpu.make_async_copy(rk_hbm.at[z], rk, ld_sem.at[0]), pltpu.make_async_copy(pi_hbm, pi, ld_sem.at[1])]
    x_copy = lambda s: pltpu.make_async_copy(x_hbm.at[s], xb.at[s], x_sem.at[s])
    ct_copy = lambda s: pltpu.make_async_copy(ct_hbm.at[s], cb.at[lax.rem(s, 2)], ci_sem.at[lax.rem(s, 2)])
    out_copy = lambda s: pltpu.make_async_copy(cb.at[lax.rem(s, 2)], out_hbm.at[s], co_sem.at[lax.rem(s, 2)])
    g_copy = lambda s: pltpu.make_async_copy(xb.at[s], gb_hbm.at[s], g_sem.at[s])

    barrier = pltpu.get_barrier_semaphore()

    def greet(d, carry):
        peer = lax.rem(me + d, nb)
        pl.semaphore_signal(barrier, inc=1, device_id=(peer, z), device_id_type=MESH)
        return carry

    lax.fori_loop(1, nb, greet, 0)

    def greet_z(d, carry):
        pl.semaphore_signal(barrier, inc=1, device_id=(me, lax.rem(z + d, nz)), device_id_type=MESH)
        return carry

    lax.fori_loop(1, nz, greet_z, 0)
    x_copy(0).start()
    for one in loads:
        one.start()

    def load_x(s, carry):
        x_copy(s).start()
        return carry

    lax.fori_loop(1, S, load_x, 0)
    ct_copy(0).start()
    cols[...] = jnp.zeros_like(cols)
    gk_ref[...] = jnp.zeros_like(gk_ref)
    for one in loads:
        one.wait()

    point = point_ref[...].astype(BF16)
    kernel_t = jnp.concatenate([dot(point, pi[k, 0:K, 0:256]) for k in range(4)], axis=0)
    kt1[...] = kernel_t[:, 0:128].astype(BF16)
    ktb[...] = kernel_t[:, 128:256]
    padded = jnp.concatenate([kernel_t.astype(BF16), jnp.zeros((256 - K, 256), BF16)], axis=0)
    kernel_n = dot_nt(eye_ref[0:K, 0:256], padded)
    kk_ref[...] = kernel_n

    def expand_weights(kq, carry):
        every = master_ref[...].reshape(slots * channels, wide).astype(BF16)
        block = dot(every, pi[kq]).astype(BF16)
        for i in range(slots):
            bigw[i, pl.ds(pl.multiple_of(kq * channels, channels), channels), :] = block[
                i * channels : (i + 1) * channels
            ]
        return carry

    lax.fori_loop(0, 8, expand_weights, 0)

    def rs_copy(s, up, c, pb, rb, ssem, rsem):
        way = 0 if up else 1
        return pltpu.make_async_remote_copy(
            src_ref=pb.at[s, c], dst_ref=rb.at[s, way, c],
            send_sem=ssem.at[s, way, c], recv_sem=rsem.at[s, way, c],
            device_id=(me, z + 1 if up else z - 1), device_id_type=MESH,
        )

    def rs_hop(j, s, bufs, finish=False):
        pb, rb = bufs[0], bufs[1]
        for up in (True, False):
            place = z if up else last - z
            c = (last - j + z) if up else (z - (last - j))

            @pl.when(place <= j)
            def _():
                copy = rs_copy(s, up, c, *bufs)
                if finish:
                    copy.wait_send()
                else:
                    @pl.when(place > 0)
                    def _():
                        way = 0 if up else 1
                        copy.wait_recv()
                        pb[s, c] = (pb[s, c].astype(F32) + rb[s, way, c].astype(F32)).astype(BF16)

                    copy.start()

    def rs_final(s, bufs):
        pb, rb = bufs[0], bufs[1]
        acc[...] = pb[s, z].astype(F32)

        @pl.when(z > 0)
        def _():
            rs_copy(s, True, z, *bufs).wait_recv()
            acc[...] += rb[s, 0, z].astype(F32)

        @pl.when(z < last)
        def _():
            rs_copy(s, False, z, *bufs).wait_recv()
            acc[...] += rb[s, 1, z].astype(F32)

        return acc[...].astype(BF16)

    def ag_copy(s, up, c, gb, ssem, rsem):
        way = 0 if up else 1
        return pltpu.make_async_remote_copy(
            src_ref=gb.at[s, c], dst_ref=gb.at[s, c],
            send_sem=ssem.at[s, way, c], recv_sem=rsem.at[s, c],
            device_id=(me, z + 1 if up else z - 1), device_id_type=MESH,
        )

    def ag_hop(j, s, bufs, finish=False):
        for up in (True, False):
            c = z - j if up else z + j
            more = z < last if up else z > 0

            @pl.when((c >= 0) if up else (c <= last))
            def _():
                copy = ag_copy(s, up, c, *bufs)
                if j > 0 and not finish:
                    copy.wait_recv()

                if j < last:
                    @pl.when(more)
                    def _():
                        if finish:
                            copy.wait_send()
                        else:
                            copy.start()

    tiled = slots % 8 == 0

    def block_of(ref, s, d):
        if tiled:
            return ref.at[s, :, pl.ds(pl.multiple_of(d * slots, slots), slots)]
        return ref.at[s, d]

    def blocks_of(ref, s):
        if tiled:
            return ref.at[s, :, pl.ds(0, (nb - 1) * slots)]
        return ref.at[s, pl.ds(0, nb - 1)]

    def whole_of(ref, s):
        if tiled:
            return jnp.concatenate([ref[s, g] for g in range(wide // 128)], axis=1)
        return ref[s].reshape(nb * slots, wide)

    def put_whole(ref, s, value):
        if tiled:
            for g in range(wide // 128):
                ref[s, g] = value[:, g * 128 : (g + 1) * 128]
        else:
            ref[s] = value.reshape(nb, slots, wide)

    def slot_rows(ref, s, i):
        if tiled:
            return jnp.concatenate([ref[s, g, pl.ds(i, nb, stride=slots), :] for g in range(wide // 128)], axis=1)
        return ref[s, :, i, :]

    def put_slot_rows(ref, s, i, value):
        if tiled:
            for g in range(wide // 128):
                ref[s, g, pl.ds(i, nb, stride=slots), :] = value[:, g * 128 : (g + 1) * 128]
        else:
            ref[s, :, i, :] = value

    def exchange(s, src, dst, which):
        def send(d, carry):
            peer = lax.rem(me + d, nb)
            pltpu.make_async_remote_copy(
                src_ref=block_of(src, s, peer), dst_ref=block_of(dst, s, me),
                send_sem=a2a_s.at[which, s], recv_sem=a2a_r.at[which, s],
                device_id=(peer, z), device_id_type=MESH,
            ).start()
            return carry

        lax.fori_loop(1, nb, send, 0)
        block_of(dst, s, me)[...] = block_of(src, s, me)[...]

    def exchanged(s, src, dst, which):
        return pltpu.make_async_remote_copy(
            src_ref=blocks_of(src, s), dst_ref=blocks_of(dst, s),
            send_sem=a2a_s.at[which, s], recv_sem=a2a_r.at[which, s],
            device_id=(lax.rem(me + 1, nb), z), device_id_type=MESH,
        )

    def forward_rows(s, pb):
        res[...] = dot(rk[...], cols[...])
        for c in range(nz):
            first = res[c * M : (c + 1) * M, :]
            second = pltpu.roll(res[nz * M + c * M : nz * M + (c + 1) * M, :], 64, 1)
            pb[s, c, :, 0:128] = first[:, 0:128].astype(BF16)
            pb[s, c, :, 128:256] = (first[:, 128:256] + second[:, 0:128]).astype(BF16)
            pb[s, c, :, 256:384] = second[:, 128:256].astype(BF16)

    def inverse_rows(s, gb, base, target):
        spread = dot_nt(eye_ref[...], gb[s].reshape(nz * M, wide)).astype(BF16)
        left = jnp.concatenate([spread[0:K], spread[K:]], axis=1)
        keep = base[...]
        high = lax.broadcasted_iota(jnp.int32, (K, 128), 1) >= 64
        for n in range(H * 2 * COLUMN_MODES // 256):
            part = dot(left, rk[:, n * 256 : (n + 1) * 256])
            turned = pltpu.roll(part, 64, 1)
            for half in range(2):
                cut = slice(half * 128, half * 128 + 128)
                target[4 * n + 2 * half] = jnp.where(high, turned[:, cut], keep).astype(BF16)
                target[4 * n + 2 * half + 1] = jnp.where(high, part[:, cut], keep).astype(BF16)

    def pair_of(ref, s, p):
        return jnp.concatenate([ref[s, 2 * p], ref[s, 2 * p + 1]], axis=1)

    def stage_a(s):
        x_copy(s).wait()

        def some(blk, carry):
            for u in range(4):
                p = blk * 4 + u
                part = dot_nt(cblk_ref[...], pair_of(xb, s, p))
                cols[pl.ds(pl.multiple_of(p * 64, 64), 64), 0:K] = part.astype(BF16)
            return carry

        lax.fori_loop(0, pairs // 4, some, 0)
        forward_rows(s, pb1)

    def stage_b(s):
        exchanged(s, xs, xr, 0).wait_recv()
        for i in range(slots):
            put_slot_rows(ps, s, i, dot_nt(slot_rows(xr, s, i).astype(BF16), bigw[i]))
        exchange(s, ps, pr, 1)

    def stage_d(s):
        exchanged(s, gs, gr, 2).wait_recv()
        for i in range(slots):
            put_slot_rows(hs, s, i, dot(slot_rows(gr, s, i).astype(BF16), bigw[i]))
        exchange(s, hs, hr, 3)

    def stage_f(s, bufs, table, src, dst, which):
        put_whole(src, s, dot(perm_ref[table], rs_final(s, bufs)))
        exchange(s, src, dst, which)

    def stage_u(s, bufs, table, src, dst, which):
        exchanged(s, src, dst, which).wait_recv()
        bufs[0][s, z] = dot(perm_ref[table], whole_of(dst, s).astype(BF16)).astype(BF16)
        ag_hop(0, s, bufs)

    def stage_c(s, half):
        slot = lax.rem(s, 2)
        if half == 0:
            @pl.when(s >= 1)
            def _():
                out_copy(s - 1).wait()

            @pl.when(s + 1 < S)
            def _():
                ct_copy(s + 1).start()

            inverse_rows(s, gb1, ktb, l2)
            ct_copy(s).wait()
        f = factor[s]

        def some(blk, carry):
            for u in range(4):
                p = blk * 4 + u
                x2 = pair_of(xb, s, p)
                both = jnp.concatenate([x2, cblk_ref[...]], axis=0)
                branch = dot(jnp.concatenate([kt1[...], l2[p]], axis=1), both)
                v = f * branch
                square = v * v
                rise = 0.5 + 0.5 * jnp.tanh(v * (GELU_A + GELU_B * square))
                y = x2.astype(F32) + v * rise
                slope = rise + rise * (1.0 - rise) * (v * (2.0 * GELU_A + 6.0 * GELU_B * square))
                c2 = pair_of(cb, slot, p).astype(F32)
                g2 = (f * c2 * slope).astype(BF16)
                y = y.astype(BF16)
                for e in range(2):
                    cb[slot, 2 * p + e] = y[:, e * W : (e + 1) * W]
                    xb[s, 2 * p + e] = g2[:, e * W : (e + 1) * W]
                back = dot_nt(both, g2)
                gk_ref[...] += back[0:K]
                cols[pl.ds(pl.multiple_of(p * 64, 64), 64), 0:K] = back[K:].astype(BF16)
            return carry

        lax.fori_loop(half * (pairs // 8), (half + 1) * (pairs // 8), some, 0)
        if half == 1:
            out_copy(s).start()
            g_copy(s).start()
            forward_rows(s, pb2)

    def pa_copy(peer):
        return pltpu.make_async_remote_copy(
            src_ref=pa.at[me], dst_ref=pa.at[me], send_sem=pa_s.at[0], recv_sem=pa_r.at[0],
            device_id=(peer, z), device_id_type=MESH,
        )

    def pz_copy(peer):
        return pltpu.make_async_remote_copy(
            src_ref=pz.at[z], dst_ref=pz.at[z], send_sem=pz_s.at[0], recv_sem=pz_r.at[0],
            device_id=(me, peer), device_id_type=MESH,
        )

    def all_but_one(ref, count, ssem, rsem, device):
        rest = ref.at[pl.ds(0, count - 1)]
        return pltpu.make_async_remote_copy(
            src_ref=rest, dst_ref=rest, send_sem=ssem.at[0], recv_sem=rsem.at[0],
            device_id=device, device_id_type=MESH,
        )

    def point_first():
        left = gk_ref[...]
        total = jnp.zeros((channels, K), F32)
        for part in range(3):
            term = left.astype(BF16)
            left = left - term.astype(F32)
            turned = dot_nt(eye_ref[0:K, 0:K], term).astype(BF16)
            for k in range(4):
                total += dot_nt(turned[k * channels : (k + 1) * channels], pi[k, 0:K, 0:K])
        pa[me] = total

        def send(d, carry):
            pa_copy(lax.rem(me + d, nb)).start()
            return carry

        lax.fori_loop(1, nb, send, 0)

    def point_second():
        all_but_one(pa, nb, pa_s, pa_r, (lax.rem(me + 1, nb), z)).wait_recv()
        pz[z] = jnp.sum(pa[...], axis=0)

        def send(d, carry):
            pz_copy(lax.rem(z + d, nz)).start()
            return carry

        lax.fori_loop(1, nz, send, 0)

    def point_third():
        all_but_one(pz, nz, pz_s, pz_r, (me, lax.rem(z + 1, nz))).wait_recv()
        pg_ref[...] = jnp.sum(pz[...], axis=0)

    def slot_gradients():
        for i in range(slots):
            g_all = jnp.concatenate([slot_rows(gr, s, i) for s in range(S)], axis=0)
            x_all = jnp.concatenate([slot_rows(xr, s, i) for s in range(S)], axis=0)
            g_turned = dot_nt(eye_ref[...], g_all.astype(BF16)).astype(BF16)
            bigw[i] = dot(g_turned, x_all.astype(BF16)).astype(BF16)

        dw_ref[...] = jnp.zeros_like(dw_ref)

        def fold(kq, carry):
            rows = pl.ds(pl.multiple_of(kq * channels, channels), channels)
            block = jnp.concatenate([bigw[i, rows, :] for i in range(slots)], axis=0)
            dw_ref[...] += dot_nt(block, pi[kq]).reshape(slots, channels, wide)
            return carry

        lax.fori_loop(0, 8, fold, 0)

    rs1 = (pb1, rb1, rs1_s, rs1_r)
    rs2 = (pb2, rb2, rs2_s, rs2_r)
    ag1 = (gb1, ag1_s, ag1_r)
    ag2 = (gb2, ag2_s, ag2_r)

    schedule = []
    schedule += [(2, lambda s: ag_hop(1, s, ag1)), (3, lambda s: rs_hop(1, s, rs2)), (5, lambda s: ag_hop(2, s, ag2))]
    schedule += [(0, stage_a), (0, lambda s: rs_hop(0, s, rs1)), (4, stage_d)]
    schedule += [(2, lambda s: ag_hop(2, s, ag1)), (3, lambda s: rs_hop(2, s, rs2)), (0, lambda s: rs_hop(1, s, rs1))]
    schedule += [(1, stage_b), (5, lambda s: ag_hop(3, s, ag2))]
    schedule += [(0, lambda s: rs_hop(2, s, rs1)), (3, lambda s: stage_f(s, rs2, 2, gs, gr, 2))]
    schedule += [(4, lambda s: stage_u(s, ag2, 3, hs, hr, 3)), (2, lambda s: ag_hop(3, s, ag1)), (2, lambda s: stage_c(s, 0))]
    schedule += [(0, lambda s: stage_f(s, rs1, 0, xs, xr, 0)), (1, lambda s: stage_u(s, ag1, 1, ps, pr, 1))]
    schedule += [(4, lambda s: ag_hop(1, s, ag2)), (2, lambda s: stage_c(s, 1)), (2, lambda s: rs_hop(0, s, rs2))]
    steps = S + max(lag for lag, _ in schedule)
    at_step = {S + 2: point_first, S + 3: point_second, S + 4: slot_gradients}

    pl.semaphore_wait(barrier, nb + nz - 2)

    def iteration(t, carry):
        for lag, stage in schedule:
            s = t - lag
            pl.when((s >= 0) & (s < S))(functools.partial(stage, s))
        for step, work in at_step.items():
            pl.when(t == step)(work)
        return carry

    lax.fori_loop(0, steps, iteration, 0)
    point_third()

    def finish(s, carry):
        for j in range(last):
            rs_hop(j, s, rs1, True)
            rs_hop(j, s, rs2, True)
            ag_hop(j, s, ag1, True)
            ag_hop(j, s, ag2, True)
        for which, (src, dst) in enumerate(((xs, xr), (ps, pr), (gs, gr), (hs, hr))):
            exchanged(s, src, dst, which).wait_send()
        g_copy(s).wait()
        return carry

    lax.fori_loop(0, S, finish, 0)
    all_but_one(pa, nb, pa_s, pa_r, (lax.rem(me + 1, nb), z)).wait_send()
    all_but_one(pz, nz, pz_s, pz_r, (me, lax.rem(z + 1, nz))).wait_send()
    out_copy(S - 1).wait()


def field_gradient_kernel(
    sizes, rk_hbm, kk_ref, eye_ref, cblk_ref, gb2_ref, g_ref, ct_ref, ig_ref, rk, left, l2, sem
):
    nz, H, K, W, M, parts = sizes
    wide = 2 * K
    part = pl.program_id(1)
    z = lax.axis_index("row")

    @pl.when((pl.program_id(0) == 0) & (part == 0))
    def _():
        load = pltpu.make_async_copy(rk_hbm.at[z], rk, sem.at[0])
        load.start()
        load.wait()

    @pl.when(part == 0)
    def _():
        spread = dot_nt(eye_ref[...], gb2_ref[0].reshape(nz * M, wide)).astype(BF16)
        left[:, 0 : nz * M] = spread[0:K]
        left[:, nz * M :] = spread[K:]

    high = lax.broadcasted_iota(jnp.int32, (K, 128), 1) >= 64
    keep = kk_ref[:, 128:256]
    first = kk_ref[:, 0:128].astype(BF16)
    quads = H // 4 // parts
    span = quads * 128
    across = dot(left[...], rk[:, pl.ds(pl.multiple_of(part * span, span), span)])
    for n in range(quads // 2):
        cut = across[:, n * 256 : (n + 1) * 256]
        turned = pltpu.roll(cut, 64, 1)
        for half in range(2):
            lanes = slice(half * 128, half * 128 + 128)
            l2[4 * n + 2 * half] = jnp.where(high, turned[:, lanes], keep).astype(BF16)
            l2[4 * n + 2 * half + 1] = jnp.where(high, cut[:, lanes], keep).astype(BF16)

    for p in range(H // 2 // parts):
        pair = jnp.concatenate([g_ref[0, 2 * p], g_ref[0, 2 * p + 1]], axis=1)
        both = jnp.concatenate([pair, cblk_ref[...]], axis=0)
        y = dot(jnp.concatenate([first, l2[p]], axis=1), both)
        c2 = jnp.concatenate([ct_ref[0, 2 * p], ct_ref[0, 2 * p + 1]], axis=1)
        y = (y + c2.astype(F32)).astype(BF16)
        ig_ref[0, 2 * p] = y[:, 0:W]
        ig_ref[0, 2 * p + 1] = y[:, W : 2 * W]


def orthogonalize(matrices):
    norm_size = jnp.sqrt(jnp.sum(matrices * matrices, axis=(-2, -1), keepdims=True))
    current = matrices / (norm_size + 1e-07)
    for repeat in range(5):
        gram_matrix = jnp.einsum("...ij,...kj->...ik", current, current, precision=PRECISE)
        polynomial = QUINTIC_SECOND * gram_matrix + QUINTIC_THIRD * jnp.einsum(
            "...ij,...jk->...ik", gram_matrix, gram_matrix, precision=PRECISE
        )
        current = QUINTIC_FIRST * current + jnp.einsum(
            "...ij,...jk->...ik", polynomial, current, precision=PRECISE
        )
    return current


def per_device(
    input_field,
    cotangent,
    sample_scale,
    scale_table,
    owner_map,
    spectral_master,
    spectral_momentum,
    pointwise_master,
    pointwise_momentum,
):
    S, H, K, W = input_field.shape
    nz = lax.axis_size("row")
    nb = lax.axis_size("batch")
    z = lax.axis_index("row")
    slots = spectral_master.shape[0]
    channels = K // 4
    wide = 2 * K
    local_columns = COLUMN_MODES // nz
    M = ROW_MODES * local_columns
    grid = H * nz

    group_mode = lax.dynamic_index_in_dim(owner_map.reshape(nb, nz, slots), z, 1, False).reshape(nb * slots)
    group_local = group_mode // COLUMN_MODES * local_columns + group_mode % local_columns
    local_ids = jnp.arange(M, dtype=jnp.int32)
    to_slots = (group_local[:, None] == local_ids[None, :]).astype(F32)
    column = z * local_columns + local_ids % local_columns
    weight = jnp.where(column == 0, 1.0, 2.0) / (grid * grid)
    to_modes = (group_local[None, :] == local_ids[:, None]).astype(F32)
    perms = jnp.stack(
        [to_slots, to_modes * weight[:, None], to_slots * weight[None, :], to_modes]
    ).astype(BF16)
    factors = jnp.take(scale_table, sample_scale)

    anywhere = pl.BlockSpec(memory_space=pl.ANY)
    vmem = pl.BlockSpec(memory_space=pltpu.VMEM)
    exchange_shape = (S, wide // 128, nb * slots, 128) if slots % 8 == 0 else (S, nb, slots, wide)
    dma = pltpu.SemaphoreType.DMA
    row_table = jnp.asarray(row_blocks(grid, nz))
    column_rows = jnp.asarray(column_block(W))
    unit = jnp.asarray(np.eye(wide).astype(ml_dtypes.bfloat16))
    output_field, grad_branch, spectral_grad, pointwise_grad, kernel_back, grad_spectra = pl.pallas_call(
        functools.partial(layer_kernel, (nb, nz, S, H, K, W, slots, M)),
        out_shape=(
            jax.ShapeDtypeStruct(input_field.shape, BF16),
            jax.ShapeDtypeStruct(input_field.shape, BF16),
            jax.ShapeDtypeStruct(spectral_master.shape, F32),
            jax.ShapeDtypeStruct(pointwise_master.shape, F32),
            jax.ShapeDtypeStruct((K, 256), F32),
            jax.ShapeDtypeStruct((S, nz, M, wide), BF16),
        ),
        in_specs=[
            anywhere, anywhere, pl.BlockSpec(memory_space=pltpu.SMEM), anywhere, anywhere,
            vmem, vmem, vmem, vmem, vmem,
        ],
        out_specs=(anywhere, anywhere, vmem, vmem, vmem, vmem),
        scratch_shapes=[
            pltpu.VMEM((S, H, K, W), BF16),
            pltpu.VMEM((2, H, K, W), BF16),
            pltpu.VMEM((2 * nz * M, H * 2 * COLUMN_MODES), BF16),
            pltpu.VMEM((8, wide, wide), BF16),
            pltpu.VMEM((slots, wide, wide), BF16),
            pltpu.VMEM((H * 2 * COLUMN_MODES, 256), BF16),
            pltpu.VMEM((2 * nz * M, 256), F32),
            pltpu.VMEM((H // 2, K, 128), BF16),
            pltpu.VMEM((K, 128), BF16),
            pltpu.VMEM((K, 128), F32),
            pltpu.VMEM((M, wide), F32),
            pltpu.VMEM((K, K), F32),
            pltpu.VMEM((nb, channels, K), F32),
            pltpu.VMEM((nz, channels, K), F32),
            pltpu.VMEM((S, nz, M, wide), BF16),
            pltpu.VMEM((S, 2, nz, M, wide), BF16),
            pltpu.VMEM((S, nz, M, wide), BF16),
            pltpu.VMEM((S, nz, M, wide), BF16),
            pltpu.VMEM((S, 2, nz, M, wide), BF16),
        ]
        + [pltpu.VMEM(exchange_shape, F32)] * 8
        + [dma((S,)), dma((S,)), dma((2,)), dma((2,)), dma((2,))]
        + [dma((1,))] * 4
        + [dma((S, 2, nz))] * 4
        + [dma((S, 2, nz)), dma((S, nz))] * 2
        + [dma((4, S))] * 2,
        compiler_params=pltpu.CompilerParams(
            collective_id=0, has_side_effects=True, vmem_limit_bytes=62 * 1024 * 1024
        ),
    )(
        input_field,
        cotangent,
        factors,
        row_table,
        jnp.asarray(product_signs(channels)),
        column_rows,
        unit,
        perms,
        spectral_master,
        pointwise_master,
    )

    parts = 2
    rows_block = pl.BlockSpec((1, H // parts, K, W), lambda s, p: (s, p, 0, 0))
    input_grad = pl.pallas_call(
        functools.partial(field_gradient_kernel, (nz, H, K, W, M, parts)),
        out_shape=jax.ShapeDtypeStruct(input_field.shape, BF16),
        grid=(S, parts),
        in_specs=[
            anywhere, vmem, vmem, vmem,
            pl.BlockSpec((1, nz, M, wide), lambda s, p: (s, 0, 0, 0)), rows_block, rows_block,
        ],
        out_specs=rows_block,
        scratch_shapes=[
            pltpu.VMEM((2 * nz * M, H * 2 * COLUMN_MODES), BF16),
            pltpu.VMEM((K, 2 * nz * M), BF16),
            pltpu.VMEM((H // 2 // parts, K, 128), BF16),
            dma((1,)),
        ],
        compiler_params=pltpu.CompilerParams(vmem_limit_bytes=48 * 1024 * 1024),
    )(row_table, kernel_back, unit, column_rows, grad_spectra, grad_branch, cotangent)

    spectral_moment = MOMENTUM_DECAY * spectral_momentum + spectral_grad
    spectral_weight = spectral_master - SPECTRAL_RATE * orthogonalize(spectral_moment)
    pointwise_moment = MOMENTUM_DECAY * pointwise_momentum + pointwise_grad
    pointwise_weight = pointwise_master - POINTWISE_RATE * orthogonalize(pointwise_moment)
    return (
        output_field,
        input_grad,
        spectral_grad,
        spectral_moment,
        spectral_weight,
        spectral_weight.astype(BF16),
        pointwise_grad,
        pointwise_moment,
        pointwise_weight,
        pointwise_weight.astype(BF16),
    )


def solution(mesh):
    return jax.shard_map(
        per_device,
        mesh=mesh,
        in_specs=(
            P("batch", "row", None, None),
            P("batch", "row", None, None),
            P("batch"),
            P(),
            P(),
            P(("batch", "row"), None, None),
            P(("batch", "row"), None, None),
            P(),
            P(),
        ),
        out_specs=(
            P("batch", "row", None, None),
            P("batch", "row", None, None),
            P(("batch", "row"), None, None),
            P(("batch", "row"), None, None),
            P(("batch", "row"), None, None),
            P(("batch", "row"), None, None),
            P(),
            P(),
            P(),
            P(),
        ),
        check_vma=False,
    )
```

time: 775 us -> 268 us (0.35)
  waiting for transfers between devices: 248 us -> 0 us
  Pallas kernels: 0 us -> 232 us
  local copies, waits for them, and re-layouts: 164 us -> 16.6 us
  matrix products: 156 us -> 13.3 us
  blocking collectives: 101 us -> 0 us
  other arithmetic: 61.6 us -> 3.51 us
  starting transfers between devices: 21.9 us -> 0 us
  between operations: 16.2 us -> 1.71 us
    pallas_call x0 -> x2, Pallas kernels: none -> 232 us  [the longest x1 208 us: per_device(): pl.pallas_call(functools.partial(layer_kernel, (nb, nz, S, H, K, W, slots...]
    all_to_all x4 -> x0, waiting for transfers between devices: 217 us -> none  [the longest x1 90.7 us: per_device(): lax.all_to_all(rows_back, 'row', split_axis=1, concat_axis=3, tiled=True)]
    dot_general x14 -> x0, matrix products: 143 us -> none  [the longest x1 37.3 us: per_device(): jnp.einsum('shkw,kj->shjw', input_field, kernel, preferred_element_type=f...]
    psum x1 -> x0, blocking collectives: 101 us -> none  [per_device(): pointwise_grad = lax.psum(local_point_grad, ('batch', 'row'))]
    reshape x17 -> x2, local copies, waits for them, and re-layouts: 63.7 us -> 0.85 us  [the longest x1 0.77 us: per_device(): owner_map.reshape(nb, nz, slots)]
    all_gather x1 -> x0, waiting for transfers between devices: 30.4 us -> none  [per_device(): lax.all_gather(spectral_master.astype(low_type), 'batch', axis=0, tiled=T...]
    all_to_all x4 -> x0, local copies, waits for them, and re-layouts: 22.5 us -> none  [the longest x1 6.65 us: per_device(): lax.all_to_all(rows_back, 'row', split_axis=1, concat_axis=3, tiled=True)]
    all_to_all x4 -> x0, starting transfers between devices: 21.6 us -> none  [the longest x1 6.45 us: per_device(): lax.all_to_all(columns, 'row', split_axis=3, concat_axis=1, tiled=True)]
  transfers between devices with their start and end apart: 6 -> 0, of which waited for: 4 -> 0; matrix products, arithmetic and copies ran while one was open for 15% -> 0% of each run, Pallas kernels for 0% -> 0%
where the time goes in v1:
time: 268 us; the launch traced here: 267 us
  Pallas kernels  232 us (87%)
  local copies, waits for them, and re-layouts  16.6 us (6%)
  matrix products  13.3 us (5%)
  other arithmetic  3.51 us (1%)
    pallas_call x1, Pallas kernels, per_device(): pl.pallas_call(functools.partial(layer_kernel, (nb, nz, S, H, K, W, slots...  208 us
    pallas_call x1, Pallas kernels, per_device(): pl.pallas_call(functools.partial(field_gradient_kernel, (nz, H, K, W, M,...  24.7 us
    unnamed x31, local copies, waits for them, and re-layouts  15.1 us
    dot_general x10, matrix products, orthogonalize(): jnp.einsum('...ij,...jk->...ik', polynomial, current, precision=PRECISE)  5.86 us

profile of v1, /device:TPU:0, one launch (start us, length us, event | category | flops | bytes accessed | tf_op | source)
XLA Modules:
  0.0 267.5 jit_solution(4998323982571282106)
XLA Ops:
  0.7 0.7 compare_select_fusion
  1.3 0.6 gather_fusion
  2.0 1.2 and_select_fusion.3.factor
  3.2 0.8 reshape.326
  4.2 0.7 pad_maximum_fusion.perm_ref
  4.9 207.8 %shard_map.204 = (bf16[8,32,192,128]{3,2,1,0:T(8,128)(2,1)}, bf16[8,32,192,128]{3,2,1,0:T(8,128)(2,1)}, f32[8,48,384]{2,1,0:T(8,128)}, f32[48,192]{1,0:T(8,128)}...) custom-call(bf16[8,32,192,128]{3,2,1,0:T(8,128)(2,1)} %x_hbm.1, bf16[8,32,192,128]{3,2,1,0:T(8,128)(2,1)} %ct_ref.1, ...), custom_call_target="tpu_custom_call" | custom-call | tf_op jit(solution)/shard_map/pallas_call | solution.py:588
  212.7 1.4 copy-done.2
  214.1 0.9 copy-done.4
  215.0 24.7 %shard_map.205 = bf16[8,32,192,128]{3,2,1,0:T(8,128)(2,1)} custom-call(bf16[4,512,1024]{2,1,0:T(8,128)(2,1)} %constant.104.clone.rk_hbm, f32[192,256]{1,0:T(8,128)S(1)} %copy-done.4, bf16[384,384]{1,0:T(8,128)(2,1)S(1)} %copy-done.3, bf16[64,256]{1,0:T(8,128)(2,1)S(1)} %copy-done.5, bf16[8,4,64,384]{3,2,1,0:T(8,128)(2,1)S(1)} %copy-done.2, ...), custom_call_target="tpu_custom_call" | custom-call | tf_op jit(solution)/shard_map/pallas_call | solution.py:648
  239.8 0.2 multiply_reduce_fusion
  240.0 0.9 fusion.14
  240.9 0.3 fusion.6
  241.2 0.7 convolution_add_fusion.4
  242.0 0.8 fusion.21
  242.8 0.3 fusion.5
  243.1 0.7 convolution_add_fusion.3
  243.8 0.8 fusion.22
  244.6 0.3 fusion.4
  244.9 0.7 convolution_add_fusion.2
  245.6 0.8 fusion.23
  246.4 0.3 fusion.3
  246.7 0.7 convolution_add_fusion.1
  247.4 0.8 fusion.24
  248.2 0.3 fusion.2
  248.5 1.6 fusion.19
  250.1 0.6 multiply_reduce_fusion.1
  251.5 0.2 fusion.15
  252.6 0.2 fusion.26
  254.0 0.8 fusion.20
  254.8 11.3 %copy.26 = bf16[8,32,192,128]{3,2,1,0:T(8,128)(2,1)} copy(bf16[8,32,192,128]{3,2,1,0:T(8,128)(2,1)} %get-tuple-element.44) | data formatting | bytes 25165824
  266.1 0.8 copy.27
  266.9 0.6 copy.28
  (46 shorter events, 2.4 us)
Async XLA Ops:
  0.6 0.7 copy-start
  4.9 207.8 %copy-start.3 = (bf16[384,384]{1,0:T(8,128)(2,1)S(1)}, bf16[384,384]{1,0:T(8,128)(2,1)}, u32[]{:S(2)}) copy-start(bf16[384,384]{1,0:T(8,128)(2,1)} %constant.106.clone.eye_ref) | copy-start | bytes 884740
  4.9 207.8 %copy-start.5 = (bf16[64,256]{1,0:T(8,128)(2,1)S(1)}, bf16[64,256]{1,0:T(8,128)(2,1)}, u32[]{:S(2)}) copy-start(bf16[64,256]{1,0:T(8,128)(2,1)} %constant.105.clone.cblk_ref) | copy-start | bytes 98308
  212.7 1.4 copy-start.2
  214.1 0.9 copy-start.4
  215.0 24.7 %copy-start.6 = (f32[8,48,384]{2,1,0:T(8,128)S(1)}, f32[8,48,384]{2,1,0:T(8,128)}, u32[]{:S(2)}) copy-start(f32[8,48,384]{2,1,0:T(8,128)} %get-tuple-element.46) | copy-start | bytes 1769476
  215.0 24.7 %copy-start.8 = (f32[8,48,384]{2,1,0:T(8,128)S(1)}, f32[8,48,384]{2,1,0:T(8,128)}, u32[]{:S(2)}) copy-start(f32[8,48,384]{2,1,0:T(8,128)} %param.19) | copy-start | bytes 1769476
  239.7 8.8 %copy-start.7 = (f32[8,48,384]{2,1,0:T(8,128)S(1)}, f32[8,48,384]{2,1,0:T(8,128)}, u32[]{:S(2)}) copy-start(f32[8,48,384]{2,1,0:T(8,128)} %master_ref.1) | copy-start | bytes 1769476
  239.7 10.4 %copy-start.11 = (f32[48,192]{1,0:T(8,128)S(1)}, f32[48,192]{1,0:T(8,128)}, u32[]{:S(2)}) copy-start(f32[48,192]{1,0:T(8,128)} %get-tuple-element.50) | copy-start | bytes 110596
  239.7 10.4 %copy-start.12 = (f32[48,192]{1,0:T(8,128)S(1)}, f32[48,192]{1,0:T(8,128)}, u32[]{:S(2)}) copy-start(f32[48,192]{1,0:T(8,128)} %param.21) | copy-start | bytes 110596
  239.7 14.3 %copy-start.10 = (f32[48,192]{1,0:T(8,128)S(1)}, f32[48,192]{1,0:T(8,128)}, u32[]{:S(2)}) copy-start(f32[48,192]{1,0:T(8,128)} %point_ref.1) | copy-start | bytes 110596
  240.0 26.1 %copy-start.9 = (f32[8,48,384]{2,1,0:T(8,128)}, f32[8,48,384]{2,1,0:T(8,128)S(1)}, u32[]{:S(2)}) copy-start(f32[8,48,384]{2,1,0:T(8,128)S(1)} %get-tuple-element.47) | copy-start | bytes 1769476
  250.8 15.3 %copy-start.13 = (f32[48,192]{1,0:T(8,128)}, f32[48,192]{1,0:T(8,128)S(1)}, u32[]{:S(2)}) copy-start(f32[48,192]{1,0:T(8,128)S(1)} %get-tuple-element.51) | copy-start | bytes 110596
  254.8 12.7 %copy-start.1 = (f32[8]{0:T(128)S(1)}, f32[8]{0:T(128)}, u32[]{:S(2)}) copy-start(f32[8]{0:T(128)} %param.16) | copy-start | bytes 100

commit v2 on v1

v2 whole, which is shorter than its diff:
```python
import functools
import math

import jax
import jax.numpy as jnp
import ml_dtypes
import numpy as np
from jax import lax
from jax.experimental import pallas as pl
from jax.experimental.pallas import tpu as pltpu
from jax.sharding import PartitionSpec as P

ROW_MODES = 16
COLUMN_MODES = 16

BLADE_SIGNS = np.array([[1, 1, 1, 1], [1, 1, 1, 1], [1, -1, 1, -1], [1, -1, 1, -1]], np.float32)
QUINTIC_FIRST = 3.4445
QUINTIC_SECOND = -4.775
QUINTIC_THIRD = 2.0315
SPECTRAL_RATE = 4.0
POINTWISE_RATE = 0.8
MOMENTUM_DECAY = 0.5
MESH = pl.DeviceIdType.MESH
F32 = jnp.float32
BF16 = jnp.bfloat16
GELU_A = math.sqrt(2.0 / math.pi)
GELU_B = GELU_A * 0.044715


MATRIX_SIGNS = np.zeros((2, 2, 4), np.float32)
MATRIX_SIGNS[0, 0, 0] = MATRIX_SIGNS[0, 0, 1] = MATRIX_SIGNS[1, 1, 0] = 1.0
MATRIX_SIGNS[1, 1, 1] = MATRIX_SIGNS[1, 0, 3] = -1.0
MATRIX_SIGNS[0, 1, 2] = MATRIX_SIGNS[0, 1, 3] = MATRIX_SIGNS[1, 0, 2] = 1.0


def column_block(grid_size, row_count):
    angles = 2.0 * np.pi / grid_size * (np.arange(COLUMN_MODES)[:, None] * np.arange(grid_size)[None] % grid_size)
    table = np.stack([np.cos(angles), -np.sin(angles)], 0).reshape(2, row_count, -1, grid_size)
    full = np.einsum("pclw,hg->chplgw", table, np.eye(2))
    return full.reshape(4 * COLUMN_MODES, 2 * grid_size).astype(ml_dtypes.bfloat16)


def row_blocks(grid_size, row_count):
    rows = grid_size // row_count
    local = COLUMN_MODES // row_count
    r = np.arange(ROW_MODES)
    frequency = np.where(r < ROW_MODES // 2, r, grid_size - ROW_MODES + r)
    angles = 2.0 * np.pi / grid_size * (frequency[:, None] * np.arange(grid_size)[None] % grid_size)
    cosine, sine = np.cos(angles), np.sin(angles)
    table = np.stack([np.stack([cosine, sine], -1), np.stack([-sine, cosine], -1)], 0)
    table = table.reshape(2, ROW_MODES, row_count, rows, 2)
    single = np.einsum("qrzhp,cd->zqrchpd", table, np.eye(local))
    single = single.reshape(row_count, 2 * ROW_MODES * local, rows * 2 * local).astype(ml_dtypes.bfloat16)
    parts = single.reshape(row_count, 2 * ROW_MODES * local, rows // 2, 4 * local)
    every = np.zeros((row_count, row_count, parts.shape[1], rows // 2, row_count, 4 * local), ml_dtypes.bfloat16)
    for group in range(row_count):
        every[:, group, :, :, group, :] = parts
    return single, every.reshape(row_count, 4 * ROW_MODES * COLUMN_MODES // 2, rows * 2 * COLUMN_MODES)


def lanes_of_columns(channels):
    half = 4 * channels
    place = np.arange(2 * half)
    cut = half // 128 * 128
    first = np.arange(half)
    second = np.where(first < cut, half + (half - cut) + first, half + first - cut)
    return place[first], place[second]


def product_signs(channels):
    unit = np.eye(channels, dtype=np.float32)
    psi = np.zeros((2, 2, 2, 4, 2, 2), np.float32)
    for q in range(2):
        for p in range(2):
            part = -1.0 if (q == 0 and p == 1) else 1.0
            for row in range(2):
                for inner in range(2):
                    psi[q, row, p ^ q, :, p, inner] = part * MATRIX_SIGNS[row, inner]
    psi = np.einsum("qrwapn,ij->qrwaipnj", psi, unit).reshape(4, 8 * channels, 4 * channels)
    psi = np.pad(psi, ((0, 0), (0, 0), (0, 256 - 4 * channels)))
    spread = np.einsum("pt,ncb,ij->pbictnj", np.eye(2), MATRIX_SIGNS, unit)
    spread = spread.reshape(8 * channels, 2, 4 * channels)
    turn = np.zeros((8 * channels, 8 * channels), np.float32)
    for col, lanes in enumerate(lanes_of_columns(channels)):
        turn[:, lanes] = spread[:, col]
    point = np.zeros((4, 4, 4), np.float32)
    for k in range(4):
        for b in range(4):
            point[k, k ^ b, b] = BLADE_SIGNS[k ^ b, b]
    point = np.einsum("kab,ij->kaibj", point, unit).reshape(4, 4 * channels, 4 * channels)
    point = np.pad(point, ((0, 0), (0, 0), (0, 256 - 4 * channels)))
    return (one.astype(ml_dtypes.bfloat16) for one in (psi, turn, point))


def dot(a, b):
    return lax.dot_general(a, b, (((1,), (0,)), ((), ())), preferred_element_type=F32)


def dot_nt(a, b):
    return lax.dot_general(a, b, (((1,), (1,)), ((), ())), preferred_element_type=F32)


def layer_kernel(
    sizes,
    x_hbm, ct_hbm, scale_ref, table_ref, owner_ref, single_hbm, every_hbm, psi_hbm, master_hbm, momentum_hbm,
    turn_ref, sign_ref, cblk_ref, eye_ref, point_ref, point_momentum_ref,
    ob, xb, dw_ref, pg_ref, turned_ref, point_turned_ref,
    eb, single, every, psi, master_ref, momentum_ref, wm, cols, l2, kt1, ktb, kk1, kkb, acc, gk_ref, pa, pz,
    lows, highs, perm_ref, back_ref,
    pb1, rb1, gb1, pb2, rb2, gb2,
    xs, xr, ps, pr, gs, gr, hs, hr,
    x_sem, ct_sem, ld_sem, ei_sem, pa_s, pa_r, pz_s, pz_r,
    rs1_s, rs1_r, rs2_s, rs2_r, ag1_s, ag1_r, ag2_s, ag2_r, a2a_s, a2a_r,
):
    nb, nz, S, H, K, W, slots, M = sizes
    wide = 2 * K
    channels = K // 4
    pairs = H // 2
    me = lax.axis_index("batch")
    z = lax.axis_index("row")
    last = nz - 1

    loads = [
        pltpu.make_async_copy(psi_hbm, psi, ld_sem.at[0]),
        pltpu.make_async_copy(single_hbm.at[z], single, ld_sem.at[1]),
        pltpu.make_async_copy(every_hbm.at[z], every, ld_sem.at[2]),
        pltpu.make_async_copy(master_hbm, master_ref, ld_sem.at[3]),
        pltpu.make_async_copy(momentum_hbm, momentum_ref, ld_sem.at[4]),
    ]
    x_copy = lambda s: pltpu.make_async_copy(x_hbm.at[s], xb.at[s], x_sem.at[s])
    ct_copy = lambda s: pltpu.make_async_copy(ct_hbm.at[s], ob.at[s], ct_sem.at[s])
    ect_copy = lambda s: pltpu.make_async_copy(ct_hbm.at[s], eb.at[lax.rem(s, 2)], ei_sem.at[lax.rem(s, 2)])

    barrier = pltpu.get_barrier_semaphore()

    def greet(d, carry):
        peer = lax.rem(me + d, nb)
        pl.semaphore_signal(barrier, inc=1, device_id=(peer, z), device_id_type=MESH)
        return carry

    lax.fori_loop(1, nb, greet, 0)

    def greet_z(d, carry):
        pl.semaphore_signal(barrier, inc=1, device_id=(me, lax.rem(z + d, nz)), device_id_type=MESH)
        return carry

    lax.fori_loop(1, nz, greet_z, 0)
    for one in loads:
        one.start()

    def load_x(s, carry):
        x_copy(s).start()
        return carry

    def load_ct(s, carry):
        ct_copy(s).start()
        return carry

    lax.fori_loop(0, S, load_x, 0)
    lax.fori_loop(0, S, load_ct, 0)
    ect_copy(0).start()
    cols[...] = jnp.zeros_like(cols)
    gk_ref[...] = jnp.zeros_like(gk_ref)
    wm[...] = jnp.zeros_like(wm)

    local = COLUMN_MODES // nz
    lane = lax.broadcasted_iota(jnp.int32, (1, 2 * M), 1)

    def place(d, carry):
        for i in range(slots):
            mode = owner_ref[(d * nz + z) * slots + i]
            at = lax.div(mode, COLUMN_MODES) * local + lax.rem(mode, local)
            lows[pl.ds(d * slots + i, 1), :] = jnp.where(lane == at, 1.0, 0.0)
            highs[pl.ds(d * slots + i, 1), :] = jnp.where(lane == at + M, 1.0, 0.0)
        return carry

    lax.fori_loop(0, nb, place, 0)
    inner = 1.0 / (H * nz * H * nz)
    weigh = jnp.where(z * local + lax.rem(lane, local) == 0, 0.5 * inner, inner)
    for table, pick in enumerate((lambda v: v[...], lambda v: v[...] * weigh)):
        perm_ref[table] = pick(lows)[:, 0:M].astype(BF16)
        back_ref[1 - table, 0] = pick(lows).astype(BF16)
        back_ref[1 - table, 1] = pick(highs).astype(BF16)

    weight = point_ref[...].astype(BF16)
    kernel_t = jnp.concatenate([dot(weight, sign_ref[k]) for k in range(4)], axis=0)
    kt1[...] = kernel_t[:, 0:128].astype(BF16)
    ktb[...] = kernel_t[:, 128:256]
    padded = jnp.concatenate([kernel_t.astype(BF16), jnp.zeros((256 - K, 256), BF16)], axis=0)
    kernel_n = dot_nt(eye_ref[0:K], padded)
    kk1[...] = kernel_n[:, 0:128].astype(BF16)
    kkb[...] = kernel_n[:, 128:256]
    for one in loads:
        one.wait()
    masters = master_ref[...].reshape(slots * channels, wide).astype(BF16)
    for part in range(4):
        block = dot(masters, psi[part]).astype(BF16)
        for i in range(slots):
            wm[i, part * channels : (part + 1) * channels, :] = block[i * channels : (i + 1) * channels]

    def rs_copy(s, up, c, pb, rb, ssem, rsem):
        way = 0 if up else 1
        return pltpu.make_async_remote_copy(
            src_ref=pb.at[s, c], dst_ref=rb.at[s, way, c],
            send_sem=ssem.at[s, way, c], recv_sem=rsem.at[s, way, c],
            device_id=(me, z + 1 if up else z - 1), device_id_type=MESH,
        )

    def rs_hop(j, s, bufs, finish=False):
        pb, rb = bufs[0], bufs[1]
        for up in (True, False):
            place = z if up else last - z
            c = (last - j + z) if up else (z - (last - j))

            @pl.when(place <= j)
            def _():
                copy = rs_copy(s, up, c, *bufs)
                if finish:
                    copy.wait_send()
                else:
                    @pl.when(place > 0)
                    def _():
                        way = 0 if up else 1
                        copy.wait_recv()
                        pb[s, c] = (pb[s, c].astype(F32) + rb[s, way, c].astype(F32)).astype(BF16)

                    copy.start()

    def rs_final(s, bufs):
        pb, rb = bufs[0], bufs[1]
        acc[...] = pb[s, z].astype(F32)

        @pl.when(z > 0)
        def _():
            rs_copy(s, True, z, *bufs).wait_recv()
            acc[...] += rb[s, 0, z].astype(F32)

        @pl.when(z < last)
        def _():
            rs_copy(s, False, z, *bufs).wait_recv()
            acc[...] += rb[s, 1, z].astype(F32)

        return acc[...].astype(BF16)

    def ag_copy(s, up, c, gb, ssem, rsem):
        way = 0 if up else 1
        return pltpu.make_async_remote_copy(
            src_ref=gb.at[s, c], dst_ref=gb.at[s, c],
            send_sem=ssem.at[s, way, c], recv_sem=rsem.at[s, c],
            device_id=(me, z + 1 if up else z - 1), device_id_type=MESH,
        )

    def ag_hop(j, s, bufs, finish=False):
        for up in (True, False):
            c = z - j if up else z + j
            more = z < last if up else z > 0

            @pl.when((c >= 0) if up else (c <= last))
            def _():
                copy = ag_copy(s, up, c, *bufs)
                if j > 0 and not finish:
                    copy.wait_recv()

                if j < last:
                    @pl.when(more)
                    def _():
                        if finish:
                            copy.wait_send()
                        else:
                            copy.start()

    tiled = slots % 8 == 0

    def block_of(ref, s, d):
        if tiled:
            return ref.at[s, :, pl.ds(pl.multiple_of(d * slots, slots), slots)]
        return ref.at[s, d]

    def blocks_of(ref, s):
        if tiled:
            return ref.at[s, :, pl.ds(0, (nb - 1) * slots)]
        return ref.at[s, pl.ds(0, nb - 1)]

    def whole_of(ref, s):
        if tiled:
            return jnp.concatenate([ref[s, g] for g in range(wide // 128)], axis=1)
        return ref[s].reshape(nb * slots, wide)

    def put_whole(ref, s, value):
        if tiled:
            for g in range(wide // 128):
                ref[s, g] = value[:, g * 128 : (g + 1) * 128]
        else:
            ref[s] = value.reshape(nb, slots, wide)

    def slot_rows(ref, s, i):
        if tiled:
            return jnp.concatenate([ref[s, g, pl.ds(i, nb, stride=slots), :] for g in range(wide // 128)], axis=1)
        return ref[s, :, i, :]

    def put_slot_rows(ref, s, i, value):
        if tiled:
            for g in range(wide // 128):
                ref[s, g, pl.ds(i, nb, stride=slots), :] = value[:, g * 128 : (g + 1) * 128]
        else:
            ref[s, :, i, :] = value

    def exchange(s, src, dst, which):
        def send(d, carry):
            peer = lax.rem(me + d, nb)
            pltpu.make_async_remote_copy(
                src_ref=block_of(src, s, peer), dst_ref=block_of(dst, s, me),
                send_sem=a2a_s.at[which, s], recv_sem=a2a_r.at[which, s],
                device_id=(peer, z), device_id_type=MESH,
            ).start()
            return carry

        lax.fori_loop(1, nb, send, 0)
        block_of(dst, s, me)[...] = block_of(src, s, me)[...]

    def exchanged(s, src, dst, which):
        return pltpu.make_async_remote_copy(
            src_ref=blocks_of(src, s), dst_ref=blocks_of(dst, s),
            send_sem=a2a_s.at[which, s], recv_sem=a2a_r.at[which, s],
            device_id=(lax.rem(me + 1, nb), z), device_id_type=MESH,
        )

    def forward_rows(s, pb):
        for c in range(nz):
            part = dot(single[...], cols[c])
            first = part[0:M]
            second = pltpu.roll(part[M:], 64, 1)
            pb[s, c, :, 0:128] = first[:, 0:128].astype(BF16)
            pb[s, c, :, 128:256] = (first[:, 128:256] + second[:, 0:128]).astype(BF16)
            pb[s, c, :, 256:384] = second[:, 128:256].astype(BF16)

    def put_columns(p, value):
        step = 4 * COLUMN_MODES // nz
        for c in range(nz):
            cols[c, pl.ds(pl.multiple_of(p * step, step), step), 0:K] = value[c * step : (c + 1) * step]

    def pair_of(ref, s, p):
        return jnp.concatenate([ref[s, 2 * p], ref[s, 2 * p + 1]], axis=1)

    def stage_a(s):
        x_copy(s).wait()

        def some(blk, carry):
            for u in range(4):
                p = blk * 4 + u
                part = dot_nt(cblk_ref[...], pair_of(xb, s, p))
                put_columns(p, part.astype(BF16))
            return carry

        lax.fori_loop(0, pairs // 4, some, 0)
        forward_rows(s, pb1)
        rs_hop(0, s, rs1)

    def by_column(ref, s, i):
        rows = slot_rows(ref, s, i)
        low, mid, top = rows[:, 0:128], rows[:, 128:256], rows[:, 256:384]
        first = jnp.concatenate([low, mid], axis=1)
        second = jnp.concatenate([top, pltpu.roll(mid, 64, 1)], axis=1)
        return jnp.concatenate([first, second], axis=0).astype(BF16)

    def put_by_column(ref, s, i, value):
        first, second = value[0:nb], value[nb:]
        mid = first[:, 128:256] + pltpu.roll(second[:, 128:256], 64, 1)
        put_slot_rows(ref, s, i, jnp.concatenate([first[:, 0:128], mid, second[:, 0:128]], axis=1))

    def stage_b(s):
        exchanged(s, xs, xr, 0).wait_recv()
        for i in range(slots):
            put_by_column(ps, s, i, dot_nt(by_column(xr, s, i), wm[i]))
        exchange(s, ps, pr, 1)

    def stage_d(s):
        exchanged(s, gs, gr, 2).wait_recv()
        for i in range(slots):
            put_by_column(hs, s, i, dot(by_column(gr, s, i), wm[i]))
        exchange(s, hs, hr, 3)

    def stage_f(s, bufs, table, src, dst, which):
        placed = dot(perm_ref[table], rs_final(s, bufs)).astype(BF16)
        put_whole(src, s, dot(placed, turn_ref[...]))
        exchange(s, src, dst, which)

    def stage_u(s, bufs, table, src, dst, which):
        exchanged(s, src, dst, which).wait_recv()
        turned = jnp.transpose(whole_of(dst, s))
        cut = K // 128 * 128
        first = turned[0:K]
        second = jnp.concatenate([turned[2 * K - cut :], turned[K : 2 * K - cut]], axis=0)
        parts = []
        for q in range(2):
            base = 2 * q * channels
            at = lambda col, row: col[base + row * channels : base + (row + 1) * channels]
            m00, m10, m01, m11 = at(first, 0), at(first, 1), at(second, 0), at(second, 1)
            parts.append(jnp.concatenate([m00 + m11, m00 - m11, m01 + m10, m01 - m10], axis=0).astype(BF16))
        both = dot(parts[0], back_ref[table, 0]) + dot(parts[1], back_ref[table, 1])
        bufs[0][s, z] = both.astype(BF16)
        ag_hop(0, s, bufs)

    def inverse_rows(s, gb, base):
        left = jnp.concatenate([gb[s, c] for c in range(nz)], axis=1)
        keep = base[...]
        high = lax.broadcasted_iota(jnp.int32, (K, 128), 1) >= 64
        for n in range(pairs // 4):
            part = dot(left, every[:, n * 256 : (n + 1) * 256])
            turned = pltpu.roll(part, 64, 1)
            for half in range(2):
                cut = slice(half * 128, half * 128 + 128)
                l2[4 * n + 2 * half] = jnp.where(high, turned[:, cut], keep).astype(BF16)
                l2[4 * n + 2 * half + 1] = jnp.where(high, part[:, cut], keep).astype(BF16)

    def stage_c(s):
        ag_hop(last, s, ag1)
        inverse_rows(s, gb1, ktb)
        ct_copy(s).wait()
        f = table_ref[scale_ref[s]]

        def some(blk, carry):
            for u in range(4):
                p = blk * 4 + u
                x2 = pair_of(xb, s, p)
                both = jnp.concatenate([x2, cblk_ref[...]], axis=0)
                branch = dot(jnp.concatenate([kt1[...], l2[p]], axis=1), both)
                v = f * branch
                square = v * v
                rise = 0.5 + 0.5 * jnp.tanh(v * (GELU_A + GELU_B * square))
                y = x2.astype(F32) + v * rise
                slope = rise + rise * (1.0 - rise) * (v * (2.0 * GELU_A + 6.0 * GELU_B * square))
                c2 = pair_of(ob, s, p).astype(F32)
                g2 = (f * c2 * slope).astype(BF16)
                y = y.astype(BF16)
                for e in range(2):
                    ob[s, 2 * p + e] = y[:, e * W : (e + 1) * W]
                    xb[s, 2 * p + e] = g2[:, e * W : (e + 1) * W]
                back = dot_nt(both, g2)
                gk_ref[...] += back[0:K]
                put_columns(p, back[K:].astype(BF16))
            return carry

        lax.fori_loop(0, pairs // 4, some, 0)
        forward_rows(s, pb2)
        rs_hop(0, s, rs2)

    def stage_e(s):
        slot = lax.rem(s, 2)

        @pl.when(s + 1 < S)
        def _():
            ect_copy(s + 1).start()

        ag_hop(last, s, ag2)
        inverse_rows(s, gb2, kkb)
        ect_copy(s).wait()

        def some(blk, carry):
            for u in range(4):
                p = blk * 4 + u
                both = jnp.concatenate([pair_of(xb, s, p), cblk_ref[...]], axis=0)
                y = dot(jnp.concatenate([kk1[...], l2[p]], axis=1), both)
                y = (y + pair_of(eb, slot, p).astype(F32)).astype(BF16)
                for e in range(2):
                    xb[s, 2 * p + e] = y[:, e * W : (e + 1) * W]
            return carry

        lax.fori_loop(0, pairs // 4, some, 0)

    def pa_copy(peer):
        return pltpu.make_async_remote_copy(
            src_ref=pa.at[me], dst_ref=pa.at[me], send_sem=pa_s.at[0], recv_sem=pa_r.at[0],
            device_id=(peer, z), device_id_type=MESH,
        )

    def pz_copy(peer):
        return pltpu.make_async_remote_copy(
            src_ref=pz.at[z], dst_ref=pz.at[z], send_sem=pz_s.at[0], recv_sem=pz_r.at[0],
            device_id=(me, peer), device_id_type=MESH,
        )

    def all_but_one(ref, count, ssem, rsem, device):
        rest = ref.at[pl.ds(0, count - 1)]
        return pltpu.make_async_remote_copy(
            src_ref=rest, dst_ref=rest, send_sem=ssem.at[0], recv_sem=rsem.at[0],
            device_id=device, device_id_type=MESH,
        )

    def point_first():
        left = gk_ref[...]
        total = jnp.zeros((channels, K), F32)
        for part in range(3):
            term = left.astype(BF16)
            left = left - term.astype(F32)
            turned = dot_nt(eye_ref[0:K, 0:K], term).astype(BF16)
            for k in range(4):
                total += dot_nt(turned[k * channels : (k + 1) * channels], sign_ref[k, :, 0:K])
        pa[me] = total

        def send(d, carry):
            pa_copy(lax.rem(me + d, nb)).start()
            return carry

        lax.fori_loop(1, nb, send, 0)

    def point_second():
        all_but_one(pa, nb, pa_s, pa_r, (lax.rem(me + 1, nb), z)).wait_recv()
        pz[z] = jnp.sum(pa[...], axis=0)

        def send(d, carry):
            pz_copy(lax.rem(z + d, nz)).start()
            return carry

        lax.fori_loop(1, nz, send, 0)

    def slot_gradients():
        for i in range(slots):
            g_all = jnp.concatenate([by_column(gr, s, i) for s in range(S)], axis=0)
            x_all = jnp.concatenate([by_column(xr, s, i) for s in range(S)], axis=0)
            g_turned = dot_nt(eye_ref[...], g_all).astype(BF16)
            wm[i] = dot(g_turned, x_all).astype(BF16)

        total = jnp.zeros((slots * channels, wide), F32)
        for part in range(4):
            rows = slice(part * channels, (part + 1) * channels)
            block = jnp.concatenate([wm[i, rows, :] for i in range(slots)], axis=0)
            total += dot_nt(block, psi[part])
        dw_ref[...] = total.reshape(slots, channels, wide)

    def orthogonal(moments):
        def split(v):
            high = v.astype(BF16)
            return high, (v - high.astype(F32)).astype(BF16)

        def product(a, b, mul):
            (ah, al), (bh, bl) = a, b
            return mul(ah, bh) + (mul(ah, bl) + mul(al, bh))

        current = [m / (jnp.sqrt(jnp.sum(m * m)) + 1e-07) for m in moments]
        for repeat in range(5):
            parts = [split(v) for v in current]
            grams = [product(v, v, dot_nt) for v in parts]
            gram_parts = [split(v) for v in grams]
            squares = [product(v, v, dot) for v in gram_parts]
            polynomials = [split(QUINTIC_SECOND * g + QUINTIC_THIRD * q) for g, q in zip(grams, squares)]
            current = [
                QUINTIC_FIRST * v + product(p, w, dot) for v, p, w in zip(current, polynomials, parts)
            ]
        return current

    def slot_updates(chosen):
        moments = [MOMENTUM_DECAY * momentum_ref[i] + dw_ref[i] for i in chosen]
        for i, value in zip(chosen, orthogonal(moments)):
            turned_ref[i] = value

    def point_update():
        all_but_one(pz, nz, pz_s, pz_r, (me, lax.rem(z + 1, nz))).wait_recv()
        total = jnp.sum(pz[...], axis=0)
        pg_ref[...] = total
        (point_turned_ref[...],) = orthogonal([MOMENTUM_DECAY * point_momentum_ref[...] + total])

    rs1 = (pb1, rb1, rs1_s, rs1_r)
    rs2 = (pb2, rb2, rs2_s, rs2_r)
    ag1 = (gb1, ag1_s, ag1_r)
    ag2 = (gb2, ag2_s, ag2_r)

    schedule = [
        (0, stage_a),
        (3, lambda s: stage_f(s, rs1, 0, xs, xr, 0)),
        (11, lambda s: stage_f(s, rs2, 1, gs, gr, 2)),
        (2, lambda s: rs_hop(2, s, rs1)),
        (10, lambda s: rs_hop(2, s, rs2)),
        (1, lambda s: rs_hop(1, s, rs1)),
        (9, lambda s: rs_hop(1, s, rs2)),
        (7, lambda s: ag_hop(2, s, ag1)),
        (15, lambda s: ag_hop(2, s, ag2)),
        (6, lambda s: ag_hop(1, s, ag1)),
        (14, lambda s: ag_hop(1, s, ag2)),
        (5, lambda s: stage_u(s, ag1, 0, ps, pr, 1)),
        (13, lambda s: stage_u(s, ag2, 1, hs, hr, 3)),
        (4, stage_b),
        (12, stage_d),
        (8, stage_c),
        (16, stage_e),
    ]
    steps = S + max(lag for lag, _ in schedule)
    at_step = {S + 8: point_first, S + 9: point_second, S + 11: point_update, S + 12: slot_gradients}
    groups = [range(slots)[: slots // 2], range(slots)[slots // 2 :]]
    for step, group in enumerate(groups):
        if group:
            at_step[S + 13 + step] = functools.partial(slot_updates, group)

    pl.semaphore_wait(barrier, nb + nz - 2)

    def iteration(t, carry):
        for lag, stage in schedule:
            s = t - lag
            pl.when((s >= 0) & (s < S))(functools.partial(stage, s))
        for step, work in at_step.items():
            pl.when(t == step)(work)
        return carry

    lax.fori_loop(0, steps, iteration, 0)

    def finish(s, carry):
        for j in range(last):
            rs_hop(j, s, rs1, True)
            rs_hop(j, s, rs2, True)
            ag_hop(j, s, ag1, True)
            ag_hop(j, s, ag2, True)
        for which, (src, dst) in enumerate(((xs, xr), (ps, pr), (gs, gr), (hs, hr))):
            exchanged(s, src, dst, which).wait_send()
        return carry

    lax.fori_loop(0, S, finish, 0)
    all_but_one(pa, nb, pa_s, pa_r, (lax.rem(me + 1, nb), z)).wait_send()
    all_but_one(pz, nz, pz_s, pz_r, (me, lax.rem(z + 1, nz))).wait_send()


def store_kernel(
    ob, xb, dw_ref, pg_ref, turned_ref, point_turned_ref, master_ref, momentum_ref, point_ref, point_momentum_ref,
    out_hbm, ig_hbm, grad_ref, moment_ref, weight_ref, low_ref,
    point_grad_ref, point_moment_ref, point_weight_ref, point_low_ref, sem,
):
    S = ob.shape[0]
    copies = []
    for s in range(S):
        copies.append(pltpu.make_async_copy(ob.at[s], out_hbm.at[s], sem.at[0, s]))
        copies.append(pltpu.make_async_copy(xb.at[s], ig_hbm.at[s], sem.at[1, s]))
    for copy in copies:
        copy.start()
    point_grad_ref[...] = pg_ref[...]
    point_moment_ref[...] = MOMENTUM_DECAY * point_momentum_ref[...] + pg_ref[...]
    point_weight = point_ref[...] - POINTWISE_RATE * point_turned_ref[...]
    point_weight_ref[...] = point_weight
    point_low_ref[...] = point_weight.astype(BF16)
    grad_ref[...] = dw_ref[...]
    moment_ref[...] = MOMENTUM_DECAY * momentum_ref[...] + dw_ref[...]
    weight = master_ref[...] - SPECTRAL_RATE * turned_ref[...]
    weight_ref[...] = weight
    low_ref[...] = weight.astype(BF16)
    for copy in copies:
        copy.wait()


def per_device(
    input_field,
    cotangent,
    sample_scale,
    scale_table,
    owner_map,
    spectral_master,
    spectral_momentum,
    pointwise_master,
    pointwise_momentum,
):
    S, H, K, W = input_field.shape
    nz = lax.axis_size("row")
    nb = lax.axis_size("batch")
    slots = spectral_master.shape[0]
    channels = K // 4
    wide = 2 * K
    local_columns = COLUMN_MODES // nz
    M = ROW_MODES * local_columns
    grid = H * nz

    anywhere = pl.BlockSpec(memory_space=pltpu.HBM)
    smem = pl.BlockSpec(memory_space=pltpu.SMEM)
    vmem = pl.BlockSpec(memory_space=pltpu.VMEM)
    exchange_shape = (S, wide // 128, nb * slots, 128) if slots % 8 == 0 else (S, nb, slots, wide)
    dma = pltpu.SemaphoreType.DMA
    single, every = (jnp.asarray(one) for one in row_blocks(grid, nz))
    psi, turn, signs = (jnp.asarray(one) for one in product_signs(channels))
    column_rows = jnp.asarray(column_block(W, nz))
    unit = jnp.asarray(np.eye(256).astype(ml_dtypes.bfloat16))
    slot_shape, point_shape = spectral_master.shape, pointwise_master.shape
    kept = pl.pallas_call(
        functools.partial(layer_kernel, (nb, nz, S, H, K, W, slots, M)),
        out_shape=(
            pltpu.VMEM(input_field.shape, BF16),
            pltpu.VMEM(input_field.shape, BF16),
            pltpu.VMEM(slot_shape, F32),
            pltpu.VMEM(point_shape, F32),
            pltpu.VMEM(slot_shape, F32),
            pltpu.VMEM(point_shape, F32),
        ),
        in_specs=[anywhere, anywhere, smem, smem, smem] + [anywhere] * 5 + [vmem] * 6,
        out_specs=(vmem,) * 6,
        scratch_shapes=[
            pltpu.VMEM((2, H, K, W), BF16),
            pltpu.VMEM(single.shape[1:], BF16),
            pltpu.VMEM(every.shape[1:], BF16),
            pltpu.VMEM(psi.shape, BF16),
            pltpu.VMEM(spectral_master.shape, F32),
            pltpu.VMEM(spectral_master.shape, F32),
            pltpu.VMEM((slots, 256, 256), BF16),
            pltpu.VMEM((nz, single.shape[2], 256), BF16),
            pltpu.VMEM((H // 2, K, 128), BF16),
            pltpu.VMEM((K, 128), BF16),
            pltpu.VMEM((K, 128), F32),
            pltpu.VMEM((K, 128), BF16),
            pltpu.VMEM((K, 128), F32),
            pltpu.VMEM((M, wide), F32),
            pltpu.VMEM((K, K), F32),
            pltpu.VMEM((nb, channels, K), F32),
            pltpu.VMEM((nz, channels, K), F32),
            pltpu.VMEM((M, 2 * M), F32),
            pltpu.VMEM((M, 2 * M), F32),
            pltpu.VMEM((2, M, M), BF16),
            pltpu.VMEM((2, 2, M, 2 * M), BF16),
            pltpu.VMEM((S, nz, M, wide), BF16),
            pltpu.VMEM((S, 2, nz, M, wide), BF16),
            pltpu.VMEM((S, nz, K, 2 * M), BF16),
            pltpu.VMEM((S, nz, M, wide), BF16),
            pltpu.VMEM((S, 2, nz, M, wide), BF16),
            pltpu.VMEM((S, nz, K, 2 * M), BF16),
        ]
        + [pltpu.VMEM(exchange_shape, F32)] * 8
        + [dma((S,)), dma((S,)), dma((5,)), dma((2,))]
        + [dma((1,))] * 4
        + [dma((S, 2, nz))] * 4
        + [dma((S, 2, nz)), dma((S, nz))] * 2
        + [dma((4, S))] * 2,
        compiler_params=pltpu.CompilerParams(
            collective_id=0, has_side_effects=True, vmem_limit_bytes=37 * 1024 * 1024
        ),
    )(
        input_field, cotangent, sample_scale, scale_table, owner_map, single, every, psi,
        spectral_master, spectral_momentum, turn, signs, column_rows, unit, pointwise_master, pointwise_momentum,
    )

    held = [pltpu.with_memory_space_constraint(one, pltpu.VMEM) for one in kept]
    input_shape = jax.ShapeDtypeStruct(input_field.shape, BF16)
    results = pl.pallas_call(
        store_kernel,
        out_shape=(
            input_shape,
            input_shape,
            jax.ShapeDtypeStruct(slot_shape, F32),
            jax.ShapeDtypeStruct(slot_shape, F32),
            jax.ShapeDtypeStruct(slot_shape, F32),
            jax.ShapeDtypeStruct(slot_shape, BF16),
            jax.ShapeDtypeStruct(point_shape, F32),
            jax.ShapeDtypeStruct(point_shape, F32),
            jax.ShapeDtypeStruct(point_shape, F32),
            jax.ShapeDtypeStruct(point_shape, BF16),
        ),
        in_specs=[vmem] * 10,
        out_specs=(anywhere, anywhere) + (vmem,) * 8,
        scratch_shapes=[dma((2, S))],
        compiler_params=pltpu.CompilerParams(vmem_limit_bytes=6 * 1024 * 1024),
    )(*held, spectral_master, spectral_momentum, pointwise_master, pointwise_momentum)
    return tuple(results)


def solution(mesh):
    return jax.shard_map(
        per_device,
        mesh=mesh,
        in_specs=(
            P("batch", "row", None, None),
            P("batch", "row", None, None),
            P("batch"),
            P(),
            P(),
            P(("batch", "row"), None, None),
            P(("batch", "row"), None, None),
            P(),
            P(),
        ),
        out_specs=(
            P("batch", "row", None, None),
            P("batch", "row", None, None),
            P(("batch", "row"), None, None),
            P(("batch", "row"), None, None),
            P(("batch", "row"), None, None),
            P(("batch", "row"), None, None),
            P(),
            P(),
            P(),
            P(),
        ),
        check_vma=False,
    )
```

time: 268 us -> 149 us (0.56)
  Pallas kernels: 232 us -> 148 us
  local copies, waits for them, and re-layouts: 16.6 us -> 0.02 us
  matrix products: 13.3 us -> 0 us
  other arithmetic: 3.51 us -> 0 us
    pallas_call x1, Pallas kernels: 208 us -> 138 us  [per_device(): pl.pallas_call(functools.partial(layer_kernel, (nb, nz, S, H, K, W, slots...]
    unnamed x31 -> x8, local copies, waits for them, and re-layouts: 15.1 us -> 0.02 us
    pallas_call x1, Pallas kernels: 24.7 us -> 9.86 us  [per_device(): pl.pallas_call(store_kernel, out_shape=(input_shape, input_shape, jax.Sha...]
    dot_general x30 -> x0, matrix products: 13.3 us -> none  [the longest x10 5.86 us: orthogonalize(): jnp.einsum('...ij,...jk->...ik', polynomial, current, precision=PRECISE)]
where the time goes in v2:
time: 149 us
  Pallas kernels  148 us (99%)
    pallas_call x1, Pallas kernels, per_device(): pl.pallas_call(functools.partial(layer_kernel, (nb, nz, S, H, K, W, slots...  138 us
    pallas_call x1, Pallas kernels, per_device(): pl.pallas_call(store_kernel, out_shape=(input_shape, input_shape, jax.Sha...  9.86 us

profile of v2, /device:TPU:0, one launch (start us, length us, event | category | flops | bytes accessed | tf_op | source)
XLA Modules:
  0.0 148.8 jit_solution(9094021605709461657)
XLA Ops:
  0.6 0.0 copy-start.3
  0.7 0.0 copy-start.2
  0.7 0.0 copy-start.1
  0.7 0.0 copy-start
  0.7 138.2 %shard_map.231 = (bf16[8,32,192,128]{3,2,1,0:T(8,128)(2,1)S(1)}, bf16[8,32,192,128]{3,2,1,0:T(8,128)(2,1)S(1)}, f32[8,48,384]{2,1,0:T(8,128)S(1)}, f32[48,192]{1...) custom-call(bf16[8,32,192,128]{3,2,1,0:T(8,128)(2,1)} %x_hbm.1, bf16[8,32,192,128]{3,2,1,0:T(8,128)(2,1)} %ct_hbm.1, ...), custom_call_target="tpu_custom_call" | custom-call | tf_op jit(solution)/shard_map/pallas_call | solution.py:678
  138.9 0.0 copy-done.3
  138.9 0.0 copy-done.2
  138.9 0.0 copy-done.1
  138.9 0.0 copy-done
  138.9 9.9 %shard_map.232 = (bf16[8,32,192,128]{3,2,1,0:T(8,128)(2,1)}, bf16[8,32,192,128]{3,2,1,0:T(8,128)(2,1)}, f32[8,48,384]{2,1,0:T(8,128)}, f32[8,48,384]{2,1,0:T(8,1...) custom-call(bf16[8,32,192,128]{3,2,1,0:T(8,128)(2,1)S(1)} %get-tuple, ...), custom_call_target="tpu_custom_call" | custom-call | tf_op jit(solution)/shard_map/pallas_call | solution.py:735
Async XLA Ops:
  0.6 138.2 %copy-start.3 = (f32[48,192]{1,0:T(8,128)S(1)}, f32[48,192]{1,0:T(8,128)}, u32[]{:S(2)}) copy-start(f32[48,192]{1,0:T(8,128)} %point_momentum_ref.3) | copy-start | bytes 110596
  0.7 138.2 %copy-start.2 = (f32[48,192]{1,0:T(8,128)S(1)}, f32[48,192]{1,0:T(8,128)}, u32[]{:S(2)}) copy-start(f32[48,192]{1,0:T(8,128)} %point_ref.3) | copy-start | bytes 110596
  0.7 138.2 %copy-start.1 = (f32[8,48,384]{2,1,0:T(8,128)S(1)}, f32[8,48,384]{2,1,0:T(8,128)}, u32[]{:S(2)}) copy-start(f32[8,48,384]{2,1,0:T(8,128)} %momentum_ref.1) | copy-start | bytes 1769476
  0.7 138.2 %copy-start = (f32[8,48,384]{2,1,0:T(8,128)S(1)}, f32[8,48,384]{2,1,0:T(8,128)}, u32[]{:S(2)}) copy-start(f32[8,48,384]{2,1,0:T(8,128)} %master_ref.1) | copy-start | bytes 1769476

commit v3 on v2

--- a/solution.py
+++ b/solution.py
@@ -49,13 +49,8 @@
     cosine, sine = np.cos(angles), np.sin(angles)
     table = np.stack([np.stack([cosine, sine], -1), np.stack([-sine, cosine], -1)], 0)
     table = table.reshape(2, ROW_MODES, row_count, rows, 2)
-    single = np.einsum("qrzhp,cd->zqrchpd", table, np.eye(local))
-    single = single.reshape(row_count, 2 * ROW_MODES * local, rows * 2 * local).astype(ml_dtypes.bfloat16)
-    parts = single.reshape(row_count, 2 * ROW_MODES * local, rows // 2, 4 * local)
-    every = np.zeros((row_count, row_count, parts.shape[1], rows // 2, row_count, 4 * local), ml_dtypes.bfloat16)
-    for group in range(row_count):
-        every[:, group, :, :, group, :] = parts
-    return single, every.reshape(row_count, 4 * ROW_MODES * COLUMN_MODES // 2, rows * 2 * COLUMN_MODES)
+    full = np.einsum("qrzhp,cd->zqrchpd", table, np.eye(local))
+    return full.reshape(row_count, 2 * ROW_MODES * local, rows * 2 * local).astype(ml_dtypes.bfloat16)
 
 
 def lanes_of_columns(channels):
@@ -102,10 +97,10 @@
 
 def layer_kernel(
     sizes,
-    x_hbm, ct_hbm, scale_ref, table_ref, owner_ref, single_hbm, every_hbm, psi_hbm, master_hbm, momentum_hbm,
+    x_hbm, ct_hbm, scale_ref, table_ref, owner_ref, single_hbm, psi_hbm, master_hbm, momentum_hbm,
     turn_ref, sign_ref, cblk_ref, eye_ref, point_ref, point_momentum_ref,
     ob, xb, dw_ref, pg_ref, turned_ref, point_turned_ref,
-    eb, single, every, psi, master_ref, momentum_ref, wm, cols, l2, kt1, ktb, kk1, kkb, acc, gk_ref, pa, pz,
+    eb, single, psi, master_ref, momentum_ref, wm, cols, l2, kt1, ktb, kk1, kkb, acc, gk_ref, pa, pz,
     lows, highs, perm_ref, back_ref,
     pb1, rb1, gb1, pb2, rb2, gb2,
     xs, xr, ps, pr, gs, gr, hs, hr,
@@ -123,9 +118,8 @@
     loads = [
         pltpu.make_async_copy(psi_hbm, psi, ld_sem.at[0]),
         pltpu.make_async_copy(single_hbm.at[z], single, ld_sem.at[1]),
-        pltpu.make_async_copy(every_hbm.at[z], every, ld_sem.at[2]),
-        pltpu.make_async_copy(master_hbm, master_ref, ld_sem.at[3]),
-        pltpu.make_async_copy(momentum_hbm, momentum_ref, ld_sem.at[4]),
+        pltpu.make_async_copy(master_hbm, master_ref, ld_sem.at[2]),
+        pltpu.make_async_copy(momentum_hbm, momentum_ref, ld_sem.at[3]),
     ]
     x_copy = lambda s: pltpu.make_async_copy(x_hbm.at[s], xb.at[s], x_sem.at[s])
     ct_copy = lambda s: pltpu.make_async_copy(ct_hbm.at[s], ob.at[s], ct_sem.at[s])
@@ -185,11 +179,13 @@
     weight = point_ref[...].astype(BF16)
     kernel_t = jnp.concatenate([dot(weight, sign_ref[k]) for k in range(4)], axis=0)
     kt1[...] = kernel_t[:, 0:128].astype(BF16)
-    ktb[...] = kernel_t[:, 128:256]
+    for turn in range(8):
+        ktb[turn] = pltpu.roll(kernel_t[:, 128:256], (64 + 16 * turn) % 128, 1)
     padded = jnp.concatenate([kernel_t.astype(BF16), jnp.zeros((256 - K, 256), BF16)], axis=0)
     kernel_n = dot_nt(eye_ref[0:K], padded)
     kk1[...] = kernel_n[:, 0:128].astype(BF16)
-    kkb[...] = kernel_n[:, 128:256]
+    for turn in range(8):
+        kkb[turn] = pltpu.roll(kernel_n[:, 128:256], (64 + 16 * turn) % 128, 1)
     for one in loads:
         one.wait()
     masters = master_ref[...].reshape(slots * channels, wide).astype(BF16)
@@ -346,13 +342,13 @@
         x_copy(s).wait()
 
         def some(blk, carry):
-            for u in range(4):
-                p = blk * 4 + u
+            for u in range(8):
+                p = blk * 8 + u
                 part = dot_nt(cblk_ref[...], pair_of(xb, s, p))
                 put_columns(p, part.astype(BF16))
             return carry
 
-        lax.fori_loop(0, pairs // 4, some, 0)
+        lax.fori_loop(0, pairs // 8, some, 0)
         forward_rows(s, pb1)
         rs_hop(0, s, rs1)
 
@@ -402,16 +398,25 @@
         ag_hop(0, s, bufs)
 
     def inverse_rows(s, gb, base):
-        left = jnp.concatenate([gb[s, c] for c in range(nz)], axis=1)
-        keep = base[...]
-        high = lax.broadcasted_iota(jnp.int32, (K, 128), 1) >= 64
-        for n in range(pairs // 4):
-            part = dot(left, every[:, n * 256 : (n + 1) * 256])
-            turned = pltpu.roll(part, 64, 1)
-            for half in range(2):
-                cut = slice(half * 128, half * 128 + 128)
-                l2[4 * n + 2 * half] = jnp.where(high, turned[:, cut], keep).astype(BF16)
-                l2[4 * n + 2 * half + 1] = jnp.where(high, part[:, cut], keep).astype(BF16)
+        spread = dot(gb[s].reshape(nz * K, 2 * M), single[...])
+        group = lax.broadcasted_iota(jnp.int32, (K, 128), 1) // 16
+        for col in range(pairs // 8):
+            cut = slice(col * 128, col * 128 + 128)
+            parts = [spread[c * K : (c + 1) * K, cut] for c in range(nz)]
+            parts = [parts[0]] + [pltpu.roll(parts[c], 16 * c, 1) for c in range(1, nz)]
+            for first in range(4):
+                which = (group + (8 - first)) % 4
+                mixed = jnp.where(which == 0, parts[0], jnp.where(which == 1, parts[1], jnp.where(which == 2, parts[2], parts[3])))
+                for turn in (first, first + 4):
+                    inside = (group + (8 - turn)) % 8 < 4
+                    l2[col * 8 + turn] = jnp.where(inside, mixed, base[turn]).astype(BF16)
+
+    def with_columns(x2, turn):
+        rows = [x2[0:128]]
+        for g in range(8):
+            i = (g - turn) % 8
+            rows.append(cblk_ref[16 * i : 16 * i + 16, :] if i < 4 else x2[64 + 16 * i : 80 + 16 * i])
+        return jnp.concatenate(rows, axis=0)
 
     def stage_c(s):
         ag_hop(last, s, ag1)
@@ -420,28 +425,32 @@
         f = table_ref[scale_ref[s]]
 
         def some(blk, carry):
-            for u in range(4):
-                p = blk * 4 + u
+            for u in range(8):
+                p = blk * 8 + u
                 x2 = pair_of(xb, s, p)
-                both = jnp.concatenate([x2, cblk_ref[...]], axis=0)
-                branch = dot(jnp.concatenate([kt1[...], l2[p]], axis=1), both)
-                v = f * branch
-                square = v * v
-                rise = 0.5 + 0.5 * jnp.tanh(v * (GELU_A + GELU_B * square))
-                y = x2.astype(F32) + v * rise
-                slope = rise + rise * (1.0 - rise) * (v * (2.0 * GELU_A + 6.0 * GELU_B * square))
+                both = with_columns(x2, u)
+                half = (0.5 * f) * dot(jnp.concatenate([kt1[...], l2[p]], axis=1), both)
+                square = half * half
+                rise = 1.0 + jnp.tanh(half * (2.0 * GELU_A + 8.0 * GELU_B * square))
+                y = (x2.astype(F32) + half * rise).astype(BF16)
+                slope = rise + (rise * (2.0 - rise)) * (half * (2.0 * GELU_A + 24.0 * GELU_B * square))
                 c2 = pair_of(ob, s, p).astype(F32)
-                g2 = (f * c2 * slope).astype(BF16)
-                y = y.astype(BF16)
+                g2 = (((0.5 * f) * c2) * slope).astype(BF16)
                 for e in range(2):
                     ob[s, 2 * p + e] = y[:, e * W : (e + 1) * W]
                     xb[s, 2 * p + e] = g2[:, e * W : (e + 1) * W]
                 back = dot_nt(both, g2)
-                gk_ref[...] += back[0:K]
-                put_columns(p, back[K:].astype(BF16))
+                gk_ref[0:128] += back[0:128]
+                for g in range(8):
+                    i = (g - u) % 8
+                    piece = back[128 + 16 * g : 144 + 16 * g]
+                    if i < 4:
+                        cols[i, pl.ds(pl.multiple_of(p * 16, 16), 16), 0:K] = piece.astype(BF16)
+                    else:
+                        gk_ref[64 + 16 * i : 80 + 16 * i] += piece
             return carry
 
-        lax.fori_loop(0, pairs // 4, some, 0)
+        lax.fori_loop(0, pairs // 8, some, 0)
         forward_rows(s, pb2)
         rs_hop(0, s, rs2)
 
@@ -457,16 +466,16 @@
         ect_copy(s).wait()
 
         def some(blk, carry):
-            for u in range(4):
-                p = blk * 4 + u
-                both = jnp.concatenate([pair_of(xb, s, p), cblk_ref[...]], axis=0)
+            for u in range(8):
+                p = blk * 8 + u
+                both = with_columns(pair_of(xb, s, p), u)
                 y = dot(jnp.concatenate([kk1[...], l2[p]], axis=1), both)
                 y = (y + pair_of(eb, slot, p).astype(F32)).astype(BF16)
                 for e in range(2):
                     xb[s, 2 * p + e] = y[:, e * W : (e + 1) * W]
             return carry
 
-        lax.fori_loop(0, pairs // 4, some, 0)
+        lax.fori_loop(0, pairs // 8, some, 0)
 
     def pa_copy(peer):
         return pltpu.make_async_remote_copy(
@@ -670,7 +679,7 @@
     vmem = pl.BlockSpec(memory_space=pltpu.VMEM)
     exchange_shape = (S, wide // 128, nb * slots, 128) if slots % 8 == 0 else (S, nb, slots, wide)
     dma = pltpu.SemaphoreType.DMA
-    single, every = (jnp.asarray(one) for one in row_blocks(grid, nz))
+    single = jnp.asarray(row_blocks(grid, nz))
     psi, turn, signs = (jnp.asarray(one) for one in product_signs(channels))
     column_rows = jnp.asarray(column_block(W, nz))
     unit = jnp.asarray(np.eye(256).astype(ml_dtypes.bfloat16))
@@ -685,12 +694,11 @@
             pltpu.VMEM(slot_shape, F32),
             pltpu.VMEM(point_shape, F32),
         ),
-        in_specs=[anywhere, anywhere, smem, smem, smem] + [anywhere] * 5 + [vmem] * 6,
+        in_specs=[anywhere, anywhere, smem, smem, smem] + [anywhere] * 4 + [vmem] * 6,
         out_specs=(vmem,) * 6,
         scratch_shapes=[
             pltpu.VMEM((2, H, K, W), BF16),
             pltpu.VMEM(single.shape[1:], BF16),
-            pltpu.VMEM(every.shape[1:], BF16),
             pltpu.VMEM(psi.shape, BF16),
             pltpu.VMEM(spectral_master.shape, F32),
             pltpu.VMEM(spectral_master.shape, F32),
@@ -698,9 +706,9 @@
             pltpu.VMEM((nz, single.shape[2], 256), BF16),
             pltpu.VMEM((H // 2, K, 128), BF16),
             pltpu.VMEM((K, 128), BF16),
-            pltpu.VMEM((K, 128), F32),
+            pltpu.VMEM((8, K, 128), F32),
             pltpu.VMEM((K, 128), BF16),
-            pltpu.VMEM((K, 128), F32),
+            pltpu.VMEM((8, K, 128), F32),
             pltpu.VMEM((M, wide), F32),
             pltpu.VMEM((K, K), F32),
             pltpu.VMEM((nb, channels, K), F32),
@@ -717,7 +725,7 @@
             pltpu.VMEM((S, nz, K, 2 * M), BF16),
         ]
         + [pltpu.VMEM(exchange_shape, F32)] * 8
-        + [dma((S,)), dma((S,)), dma((5,)), dma((2,))]
+        + [dma((S,)), dma((S,)), dma((4,)), dma((2,))]
         + [dma((1,))] * 4
         + [dma((S, 2, nz))] * 4
         + [dma((S, 2, nz)), dma((S, nz))] * 2
@@ -726,7 +734,7 @@
             collective_id=0, has_side_effects=True, vmem_limit_bytes=37 * 1024 * 1024
         ),
     )(
-        input_field, cotangent, sample_scale, scale_table, owner_map, single, every, psi,
+        input_field, cotangent, sample_scale, scale_table, owner_map, single, psi,
         spectral_master, spectral_momentum, turn, signs, column_rows, unit, pointwise_master, pointwise_momentum,
     )
 

time: 149 us -> 145 us (0.973)
  Pallas kernels: 148 us -> 144 us
    pallas_call x1, Pallas kernels: 138 us -> 135 us  [per_device(): pl.pallas_call(functools.partial(layer_kernel, (nb, nz, S, H, K, W, slots...]
where the time goes in v3:
time: 145 us
  Pallas kernels  144 us (99%)
    pallas_call x1, Pallas kernels, per_device(): pl.pallas_call(functools.partial(layer_kernel, (nb, nz, S, H, K, W, slots...  135 us
    pallas_call x1, Pallas kernels, per_device(): pl.pallas_call(store_kernel, out_shape=(input_shape, input_shape, jax.Sha...  9.86 us

profile of v3, /device:TPU:0, one launch (start us, length us, event | category | flops | bytes accessed | tf_op | source)
XLA Modules:
  0.0 145.1 jit_solution(14892103063054851258)
XLA Ops:
  0.6 0.0 copy-start.3
  0.7 0.0 copy-start.2
  0.7 0.0 copy-start.1
  0.7 0.0 copy-start
  0.7 134.6 %shard_map.222 = (bf16[8,32,192,128]{3,2,1,0:T(8,128)(2,1)S(1)}, bf16[8,32,192,128]{3,2,1,0:T(8,128)(2,1)S(1)}, f32[8,48,384]{2,1,0:T(8,128)S(1)}, f32[48,192]{1...) custom-call(bf16[8,32,192,128]{3,2,1,0:T(8,128)(2,1)} %x_hbm.1, bf16[8,32,192,128]{3,2,1,0:T(8,128)(2,1)} %ct_hbm.1, ...), custom_call_target="tpu_custom_call" | custom-call | tf_op jit(solution)/shard_map/pallas_call | solution.py:687
  135.2 0.0 copy-done.3
  135.3 0.0 copy-done.2
  135.3 0.0 copy-done.1
  135.3 0.0 copy-done
  135.3 9.9 %shard_map.223 = (bf16[8,32,192,128]{3,2,1,0:T(8,128)(2,1)}, bf16[8,32,192,128]{3,2,1,0:T(8,128)(2,1)}, f32[8,48,384]{2,1,0:T(8,128)}, f32[8,48,384]{2,1,0:T(8,1...) custom-call(bf16[8,32,192,128]{3,2,1,0:T(8,128)(2,1)S(1)} %get-tuple, ...), custom_call_target="tpu_custom_call" | custom-call | tf_op jit(solution)/shard_map/pallas_call | solution.py:743
Async XLA Ops:
  0.6 134.6 %copy-start.3 = (f32[48,192]{1,0:T(8,128)S(1)}, f32[48,192]{1,0:T(8,128)}, u32[]{:S(2)}) copy-start(f32[48,192]{1,0:T(8,128)} %point_momentum_ref.3) | copy-start | bytes 110596
  0.7 134.6 %copy-start.2 = (f32[48,192]{1,0:T(8,128)S(1)}, f32[48,192]{1,0:T(8,128)}, u32[]{:S(2)}) copy-start(f32[48,192]{1,0:T(8,128)} %point_ref.3) | copy-start | bytes 110596
  0.7 134.6 %copy-start.1 = (f32[8,48,384]{2,1,0:T(8,128)S(1)}, f32[8,48,384]{2,1,0:T(8,128)}, u32[]{:S(2)}) copy-start(f32[8,48,384]{2,1,0:T(8,128)} %momentum_ref.1) | copy-start | bytes 1769476
  0.7 134.6 %copy-start = (f32[8,48,384]{2,1,0:T(8,128)S(1)}, f32[8,48,384]{2,1,0:T(8,128)}, u32[]{:S(2)}) copy-start(f32[8,48,384]{2,1,0:T(8,128)} %master_ref.1) | copy-start | bytes 1769476

commit v4 on v3

--- a/solution.py
+++ b/solution.py
@@ -102,10 +102,9 @@
     ob, xb, dw_ref, pg_ref, turned_ref, point_turned_ref,
     eb, single, psi, master_ref, momentum_ref, wm, cols, l2, kt1, ktb, kk1, kkb, acc, gk_ref, pa, pz,
     lows, highs, perm_ref, back_ref,
-    pb1, rb1, gb1, pb2, rb2, gb2,
-    xs, xr, ps, pr, gs, gr, hs, hr,
+    pb, rb, gb, given, taken, made, back,
     x_sem, ct_sem, ld_sem, ei_sem, pa_s, pa_r, pz_s, pz_r,
-    rs1_s, rs1_r, rs2_s, rs2_r, ag1_s, ag1_r, ag2_s, ag2_r, a2a_s, a2a_r,
+    rs_s, rs_r, ag_s, ag_r, a2a_s, a2a_r,
 ):
     nb, nz, S, H, K, W, slots, M = sizes
     wide = 2 * K
@@ -192,68 +191,67 @@
     for part in range(4):
         block = dot(masters, psi[part]).astype(BF16)
         for i in range(slots):
-            wm[i, part * channels : (part + 1) * channels, :] = block[i * channels : (i + 1) * channels]
-
-    def rs_copy(s, up, c, pb, rb, ssem, rsem):
+            wm[1, i, part * channels : (part + 1) * channels, :] = block[i * channels : (i + 1) * channels]
+    for i in range(slots):
+        wm[0, i] = dot_nt(eye_ref[...], wm[1, i]).astype(BF16)
+
+    def rs_copy(n, up, c):
         way = 0 if up else 1
         return pltpu.make_async_remote_copy(
-            src_ref=pb.at[s, c], dst_ref=rb.at[s, way, c],
-            send_sem=ssem.at[s, way, c], recv_sem=rsem.at[s, way, c],
+            src_ref=pb.at[n, c], dst_ref=rb.at[n, way, c],
+            send_sem=rs_s.at[n, way, c], recv_sem=rs_r.at[n, way, c],
             device_id=(me, z + 1 if up else z - 1), device_id_type=MESH,
         )
 
-    def rs_hop(j, s, bufs, finish=False):
-        pb, rb = bufs[0], bufs[1]
+    def rs_hop(j, n, finish=False):
         for up in (True, False):
             place = z if up else last - z
             c = (last - j + z) if up else (z - (last - j))
 
             @pl.when(place <= j)
             def _():
-                copy = rs_copy(s, up, c, *bufs)
+                copy = rs_copy(n, up, c)
                 if finish:
                     copy.wait_send()
                 else:
-                    @pl.when(place > 0)
-                    def _():
-                        way = 0 if up else 1
-                        copy.wait_recv()
-                        pb[s, c] = (pb[s, c].astype(F32) + rb[s, way, c].astype(F32)).astype(BF16)
+                    if j > 0:
+                        @pl.when(place > 0)
+                        def _():
+                            way = 0 if up else 1
+                            copy.wait_recv()
+                            pb[n, c] = (pb[n, c].astype(F32) + rb[n, way, c].astype(F32)).astype(BF16)
 
                     copy.start()
 
-    def rs_final(s, bufs):
-        pb, rb = bufs[0], bufs[1]
-        acc[...] = pb[s, z].astype(F32)
+    def rs_final(n):
+        acc[...] = pb[n, z].astype(F32)
 
         @pl.when(z > 0)
         def _():
-            rs_copy(s, True, z, *bufs).wait_recv()
-            acc[...] += rb[s, 0, z].astype(F32)
+            rs_copy(n, True, z).wait_recv()
+            acc[...] += rb[n, 0, z].astype(F32)
 
         @pl.when(z < last)
         def _():
-            rs_copy(s, False, z, *bufs).wait_recv()
-            acc[...] += rb[s, 1, z].astype(F32)
-
-        return acc[...].astype(BF16)
-
-    def ag_copy(s, up, c, gb, ssem, rsem):
+            rs_copy(n, False, z).wait_recv()
+            acc[...] += rb[n, 1, z].astype(F32)
+
+    def ag_copy(n, up, c):
         way = 0 if up else 1
         return pltpu.make_async_remote_copy(
-            src_ref=gb.at[s, c], dst_ref=gb.at[s, c],
-            send_sem=ssem.at[s, way, c], recv_sem=rsem.at[s, c],
+            src_ref=gb.at[n, c], dst_ref=gb.at[n, c],
+            send_sem=ag_s.at[n, way, c], recv_sem=ag_r.at[n, c],
             device_id=(me, z + 1 if up else z - 1), device_id_type=MESH,
         )
 
-    def ag_hop(j, s, bufs, finish=False):
+    def ag_hop(j, n, finish=False):
         for up in (True, False):
             c = z - j if up else z + j
             more = z < last if up else z > 0
 
             @pl.when((c >= 0) if up else (c <= last))
             def _():
-                copy = ag_copy(s, up, c, *bufs)
+                copy = ag_copy(n, up, c)
                 if j > 0 and not finish:
                     copy.wait_recv()
 
@@ -321,14 +319,14 @@
             device_id=(lax.rem(me + 1, nb), z), device_id_type=MESH,
         )
 
-    def forward_rows(s, pb):
+    def forward_rows(n):
         for c in range(nz):
             part = dot(single[...], cols[c])
             first = part[0:M]
             second = pltpu.roll(part[M:], 64, 1)
-            pb[s, c, :, 0:128] = first[:, 0:128].astype(BF16)
-            pb[s, c, :, 128:256] = (first[:, 128:256] + second[:, 0:128]).astype(BF16)
-            pb[s, c, :, 256:384] = second[:, 128:256].astype(BF16)
+            pb[n, c, :, 0:128] = first[:, 0:128].astype(BF16)
+            pb[n, c, :, 128:256] = (first[:, 128:256] + second[:, 0:128]).astype(BF16)
+            pb[n, c, :, 256:384] = second[:, 128:256].astype(BF16)
 
     def put_columns(p, value):
         step = 4 * COLUMN_MODES // nz
@@ -337,20 +335,6 @@
 
     def pair_of(ref, s, p):
         return jnp.concatenate([ref[s, 2 * p], ref[s, 2 * p + 1]], axis=1)
-
-    def stage_a(s):
-        x_copy(s).wait()
-
-        def some(blk, carry):
-            for u in range(8):
-                p = blk * 8 + u
-                part = dot_nt(cblk_ref[...], pair_of(xb, s, p))
-                put_columns(p, part.astype(BF16))
-            return carry
-
-        lax.fori_loop(0, pairs // 8, some, 0)
-        forward_rows(s, pb1)
-        rs_hop(0, s, rs1)
 
     def by_column(ref, s, i):
         rows = slot_rows(ref, s, i)
@@ -364,26 +348,18 @@
         mid = first[:, 128:256] + pltpu.roll(second[:, 128:256], 64, 1)
         put_slot_rows(ref, s, i, jnp.concatenate([first[:, 0:128], mid, second[:, 0:128]], axis=1))
 
-    def stage_b(s):
-        exchanged(s, xs, xr, 0).wait_recv()
+    def stage_f(n):
+        placed = dot(perm_ref[lax.div(n, S)], acc[...].astype(BF16)).astype(BF16)
+        put_whole(given, n, dot(placed, turn_ref[...]))
+
+    def stage_b(n):
+        way = lax.div(n, S)
         for i in range(slots):
-            put_by_column(ps, s, i, dot_nt(by_column(xr, s, i), wm[i]))
-        exchange(s, ps, pr, 1)
-
-    def stage_d(s):
-        exchanged(s, gs, gr, 2).wait_recv()
-        for i in range(slots):
-            put_by_column(hs, s, i, dot(by_column(gr, s, i), wm[i]))
-        exchange(s, hs, hr, 3)
-
-    def stage_f(s, bufs, table, src, dst, which):
-        placed = dot(perm_ref[table], rs_final(s, bufs)).astype(BF16)
-        put_whole(src, s, dot(placed, turn_ref[...]))
-        exchange(s, src, dst, which)
-
-    def stage_u(s, bufs, table, src, dst, which):
-        exchanged(s, src, dst, which).wait_recv()
-        turned = jnp.transpose(whole_of(dst, s))
+            put_by_column(made, n, i, dot(by_column(taken, n, i), wm[way, i]))
+
+    def stage_u(n):
+        table = lax.div(n, S)
+        turned = jnp.transpose(whole_of(back, n))
         cut = K // 128 * 128
         first = turned[0:K]
         second = jnp.concatenate([turned[2 * K - cut :], turned[K : 2 * K - cut]], axis=0)
@@ -394,11 +370,10 @@
             m00, m10, m01, m11 = at(first, 0), at(first, 1), at(second, 0), at(second, 1)
             parts.append(jnp.concatenate([m00 + m11, m00 - m11, m01 + m10, m01 - m10], axis=0).astype(BF16))
         both = dot(parts[0], back_ref[table, 0]) + dot(parts[1], back_ref[table, 1])
-        bufs[0][s, z] = both.astype(BF16)
-        ag_hop(0, s, bufs)
-
-    def inverse_rows(s, gb, base):
-        spread = dot(gb[s].reshape(nz * K, 2 * M), single[...])
+        gb[n, z] = both.astype(BF16)
+
+    def inverse_rows(n, base):
+        spread = dot(gb[n].reshape(nz * K, 2 * M), single[...])
         group = lax.broadcasted_iota(jnp.int32, (K, 128), 1) // 16
         for col in range(pairs // 8):
             cut = slice(col * 128, col * 128 + 128)
@@ -418,64 +393,47 @@
             rows.append(cblk_ref[16 * i : 16 * i + 16, :] if i < 4 else x2[64 + 16 * i : 80 + 16 * i])
         return jnp.concatenate(rows, axis=0)
 
-    def stage_c(s):
-        ag_hop(last, s, ag1)
-        inverse_rows(s, gb1, ktb)
-        ct_copy(s).wait()
+    def columns_of(s, blk):
+        for u in range(8):
+            p = blk * 8 + u
+            part = dot_nt(cblk_ref[...], pair_of(xb, s, p))
+            put_columns(p, part.astype(BF16))
+
+    def activate(s, blk):
         f = table_ref[scale_ref[s]]
-
-        def some(blk, carry):
-            for u in range(8):
-                p = blk * 8 + u
-                x2 = pair_of(xb, s, p)
-                both = with_columns(x2, u)
-                half = (0.5 * f) * dot(jnp.concatenate([kt1[...], l2[p]], axis=1), both)
-                square = half * half
-                rise = 1.0 + jnp.tanh(half * (2.0 * GELU_A + 8.0 * GELU_B * square))
-                y = (x2.astype(F32) + half * rise).astype(BF16)
-                slope = rise + (rise * (2.0 - rise)) * (half * (2.0 * GELU_A + 24.0 * GELU_B * square))
-                c2 = pair_of(ob, s, p).astype(F32)
-                g2 = (((0.5 * f) * c2) * slope).astype(BF16)
-                for e in range(2):
-                    ob[s, 2 * p + e] = y[:, e * W : (e + 1) * W]
-                    xb[s, 2 * p + e] = g2[:, e * W : (e + 1) * W]
-                back = dot_nt(both, g2)
-                gk_ref[0:128] += back[0:128]
-                for g in range(8):
-                    i = (g - u) % 8
-                    piece = back[128 + 16 * g : 144 + 16 * g]
-                    if i < 4:
-                        cols[i, pl.ds(pl.multiple_of(p * 16, 16), 16), 0:K] = piece.astype(BF16)
-                    else:
-                        gk_ref[64 + 16 * i : 80 + 16 * i] += piece
-            return carry
-
-        lax.fori_loop(0, pairs // 8, some, 0)
-        forward_rows(s, pb2)
-        rs_hop(0, s, rs2)
-
-    def stage_e(s):
+        for u in range(8):
+            p = blk * 8 + u
+            x2 = pair_of(xb, s, p)
+            both = with_columns(x2, u)
+            half = (0.5 * f) * dot(jnp.concatenate([kt1[...], l2[p]], axis=1), both)
+            square = half * half
+            rise = 1.0 + jnp.tanh(half * (2.0 * GELU_A + 8.0 * GELU_B * square))
+            y = (x2.astype(F32) + half * rise).astype(BF16)
+            slope = rise + (rise * (2.0 - rise)) * (half * (2.0 * GELU_A + 24.0 * GELU_B * square))
+            c2 = pair_of(ob, s, p).astype(F32)
+            g2 = (((0.5 * f) * c2) * slope).astype(BF16)
+            for e in range(2):
+                ob[s, 2 * p + e] = y[:, e * W : (e + 1) * W]
+                xb[s, 2 * p + e] = g2[:, e * W : (e + 1) * W]
+            down = dot_nt(both, g2)
+            gk_ref[0:128] += down[0:128]
+            for g in range(8):
+                i = (g - u) % 8
+                piece = down[128 + 16 * g : 144 + 16 * g]
+                if i < 4:
+                    cols[i, pl.ds(p * 16, 16), 0:K] = piece.astype(BF16)
+                else:
+                    gk_ref[64 + 16 * i : 80 + 16 * i] += piece
+
+    def field_gradient(s, blk):
         slot = lax.rem(s, 2)
-
-        @pl.when(s + 1 < S)
-        def _():
-            ect_copy(s + 1).start()
-
-        ag_hop(last, s, ag2)
-        inverse_rows(s, gb2, kkb)
-        ect_copy(s).wait()
-
-        def some(blk, carry):
-            for u in range(8):
-                p = blk * 8 + u
-                both = with_columns(pair_of(xb, s, p), u)
-                y = dot(jnp.concatenate([kk1[...], l2[p]], axis=1), both)
-                y = (y + pair_of(eb, slot, p).astype(F32)).astype(BF16)
-                for e in range(2):
-                    xb[s, 2 * p + e] = y[:, e * W : (e + 1) * W]
-            return carry
-
-        lax.fori_loop(0, pairs // 8, some, 0)
+        for u in range(8):
+            p = blk * 8 + u
+            both = with_columns(pair_of(xb, s, p), u)
+            y = dot(jnp.concatenate([kk1[...], l2[p]], axis=1), both)
+            y = (y + pair_of(eb, slot, p).astype(F32)).astype(BF16)
+            for e in range(2):
+                xb[s, 2 * p + e] = y[:, e * W : (e + 1) * W]
 
     def pa_copy(peer):
         return pltpu.make_async_remote_copy(
@@ -525,15 +483,15 @@
 
     def slot_gradients():
         for i in range(slots):
-            g_all = jnp.concatenate([by_column(gr, s, i) for s in range(S)], axis=0)
-            x_all = jnp.concatenate([by_column(xr, s, i) for s in range(S)], axis=0)
+            g_all = jnp.concatenate([by_column(taken, S + s, i) for s in range(S)], axis=0)
+            x_all = jnp.concatenate([by_column(taken, s, i) for s in range(S)], axis=0)
             g_turned = dot_nt(eye_ref[...], g_all).astype(BF16)
-            wm[i] = dot(g_turned, x_all).astype(BF16)
+            wm[1, i] = dot(g_turned, x_all).astype(BF16)
 
         total = jnp.zeros((slots * channels, wide), F32)
         for part in range(4):
             rows = slice(part * channels, (part + 1) * channels)
-            block = jnp.concatenate([wm[i, rows, :] for i in range(slots)], axis=0)
+            block = jnp.concatenate([wm[1, i, rows, :] for i in range(slots)], axis=0)
             total += dot_nt(block, psi[part])
         dw_ref[...] = total.reshape(slots, channels, wide)
 
@@ -569,60 +527,95 @@
         pg_ref[...] = total
         (point_turned_ref[...],) = orthogonal([MOMENTUM_DECAY * point_momentum_ref[...] + total])
 
-    rs1 = (pb1, rb1, rs1_s, rs1_r)
-    rs2 = (pb2, rb2, rs2_s, rs2_r)
-    ag1 = (gb1, ag1_s, ag1_r)
-    ag2 = (gb2, ag2_s, ag2_r)
-
-    schedule = [
-        (0, stage_a),
-        (3, lambda s: stage_f(s, rs1, 0, xs, xr, 0)),
-        (11, lambda s: stage_f(s, rs2, 1, gs, gr, 2)),
-        (2, lambda s: rs_hop(2, s, rs1)),
-        (10, lambda s: rs_hop(2, s, rs2)),
-        (1, lambda s: rs_hop(1, s, rs1)),
-        (9, lambda s: rs_hop(1, s, rs2)),
-        (7, lambda s: ag_hop(2, s, ag1)),
-        (15, lambda s: ag_hop(2, s, ag2)),
-        (6, lambda s: ag_hop(1, s, ag1)),
-        (14, lambda s: ag_hop(1, s, ag2)),
-        (5, lambda s: stage_u(s, ag1, 0, ps, pr, 1)),
-        (13, lambda s: stage_u(s, ag2, 1, hs, hr, 3)),
-        (4, stage_b),
-        (12, stage_d),
-        (8, stage_c),
-        (16, stage_e),
-    ]
-    steps = S + max(lag for lag, _ in schedule)
-    at_step = {S + 8: point_first, S + 9: point_second, S + 11: point_update, S + 12: slot_gradients}
+    at_step = {2 * S: point_first, 2 * S + 1: point_second, 2 * S + 3: slot_gradients, 2 * S + 6: point_update}
     groups = [range(slots)[: slots // 2], range(slots)[slots // 2 :]]
     for step, group in enumerate(groups):
         if group:
-            at_step[S + 13 + step] = functools.partial(slot_updates, group)
-
-    pl.semaphore_wait(barrier, nb + nz - 2)
+            at_step[2 * S + 4 + step] = functools.partial(slot_updates, group)
+    half = pairs // 8 // 2
+
+    def on(n):
+        return (n >= 0) & (n < 2 * S)
+
+    def blocks(work, s, part):
+        for blk in range(part * half, (part + 1) * half):
+            work(s, blk)
 
     def iteration(t, carry):
-        for lag, stage in schedule:
-            s = t - lag
-            pl.when((s >= 0) & (s < S))(functools.partial(stage, s))
+        starts, turns, ends = t < S, (t >= S) & (t < 2 * S), t >= 2 * S
+        pl.when(on(t - 2))(lambda: rs_hop(2, t - 2))
+        pl.when(on(t - 6))(lambda: ag_hop(2, t - 6))
+
+        @pl.when(starts)
+        def _():
+            x_copy(t).wait()
+            blocks(columns_of, t, 0)
+
+        @pl.when(turns)
+        def _():
+            ag_hop(last, t - S)
+            inverse_rows(t - S, ktb)
+            ct_copy(t - S).wait()
+            blocks(activate, t - S, 0)
+
+        @pl.when(ends)
+        def _():
+            s = t - 2 * S
+
+            @pl.when(s + 1 < S)
+            def _():
+                ect_copy(s + 1).start()
+
+            ag_hop(last, t - S)
+            inverse_rows(t - S, kkb)
+            ect_copy(s).wait()
+            blocks(field_gradient, s, 0)
+
+        pl.when(on(t - 1))(lambda: rs_hop(1, t - 1))
+        pl.when(on(t - 5))(lambda: ag_hop(1, t - 5))
+        pl.when(on(t - 3))(lambda: exchanged(t - 3, given, taken, 0).wait_recv())
+        pl.when(on(t - 4))(lambda: exchanged(t - 4, made, back, 1).wait_recv())
+
+        @pl.when(turns)
+        def _():
+            stage_u(t - 4)
+            stage_b(t - 3)
+            blocks(activate, t - S, 1)
+
+        pl.when(starts)(lambda: blocks(columns_of, t, 1))
+        pl.when(on(t - 4) & ~turns)(lambda: stage_u(t - 4))
+        pl.when(on(t - 4))(lambda: ag_hop(0, t - 4))
+        pl.when(on(t - 3) & ~turns)(lambda: stage_b(t - 3))
+        pl.when(on(t - 3))(lambda: exchange(t - 3, made, back, 1))
+        pl.when(ends)(lambda: blocks(field_gradient, t - 2 * S, 1))
+        pl.when(on(t - 2))(lambda: rs_final(t - 2))
+
+        @pl.when(turns)
+        def _():
+            stage_f(t - 2)
+            forward_rows(t)
+
+        pl.when(starts)(lambda: forward_rows(t))
+        pl.when(~ends)(lambda: rs_hop(0, t))
+        pl.when(on(t - 2) & ~turns)(lambda: stage_f(t - 2))
+        pl.when(on(t - 2))(lambda: exchange(t - 2, given, taken, 0))
         for step, work in at_step.items():
             pl.when(t == step)(work)
         return carry
 
-    lax.fori_loop(0, steps, iteration, 0)
-
-    def finish(s, carry):
+    pl.semaphore_wait(barrier, nb + nz - 2)
+
+    lax.fori_loop(0, 3 * S, iteration, 0)
+
+    def finish(n, carry):
         for j in range(last):
-            rs_hop(j, s, rs1, True)
-            rs_hop(j, s, rs2, True)
-            ag_hop(j, s, ag1, True)
-            ag_hop(j, s, ag2, True)
-        for which, (src, dst) in enumerate(((xs, xr), (ps, pr), (gs, gr), (hs, hr))):
-            exchanged(s, src, dst, which).wait_send()
+            rs_hop(j, n, True)
+            ag_hop(j, n, True)
+        exchanged(n, given, taken, 0).wait_send()
+        exchanged(n, made, back, 1).wait_send()
         return carry
 
-    lax.fori_loop(0, S, finish, 0)
+    lax.fori_loop(0, 2 * S, finish, 0)
     all_but_one(pa, nb, pa_s, pa_r, (lax.rem(me + 1, nb), z)).wait_send()
     all_but_one(pz, nz, pz_s, pz_r, (me, lax.rem(z + 1, nz))).wait_send()
 
@@ -677,7 +670,7 @@
     anywhere = pl.BlockSpec(memory_space=pltpu.HBM)
     smem = pl.BlockSpec(memory_space=pltpu.SMEM)
     vmem = pl.BlockSpec(memory_space=pltpu.VMEM)
-    exchange_shape = (S, wide // 128, nb * slots, 128) if slots % 8 == 0 else (S, nb, slots, wide)
+    exchange_shape = (2 * S, wide // 128, nb * slots, 128) if slots % 8 == 0 else (2 * S, nb, slots, wide)
     dma = pltpu.SemaphoreType.DMA
     single = jnp.asarray(row_blocks(grid, nz))
     psi, turn, signs = (jnp.asarray(one) for one in product_signs(channels))
@@ -702,7 +695,7 @@
             pltpu.VMEM(psi.shape, BF16),
             pltpu.VMEM(spectral_master.shape, F32),
             pltpu.VMEM(spectral_master.shape, F32),
-            pltpu.VMEM((slots, 256, 256), BF16),
+            pltpu.VMEM((2, slots, 256, 256), BF16),
             pltpu.VMEM((nz, single.shape[2], 256), BF16),
             pltpu.VMEM((H // 2, K, 128), BF16),
             pltpu.VMEM((K, 128), BF16),
@@ -717,19 +710,15 @@
             pltpu.VMEM((M, 2 * M), F32),
             pltpu.VMEM((2, M, M), BF16),
             pltpu.VMEM((2, 2, M, 2 * M), BF16),
-            pltpu.VMEM((S, nz, M, wide), BF16),
-            pltpu.VMEM((S, 2, nz, M, wide), BF16),
-            pltpu.VMEM((S, nz, K, 2 * M), BF16),
-            pltpu.VMEM((S, nz, M, wide), BF16),
-            pltpu.VMEM((S, 2, nz, M, wide), BF16),
-            pltpu.VMEM((S, nz, K, 2 * M), BF16),
+            pltpu.VMEM((2 * S, nz, M, wide), BF16),
+            pltpu.VMEM((2 * S, 2, nz, M, wide), BF16),
+            pltpu.VMEM((2 * S, nz, K, 2 * M), BF16),
         ]
-        + [pltpu.VMEM(exchange_shape, F32)] * 8
+        + [pltpu.VMEM(exchange_shape, F32)] * 4
         + [dma((S,)), dma((S,)), dma((4,)), dma((2,))]
         + [dma((1,))] * 4
-        + [dma((S, 2, nz))] * 4
-        + [dma((S, 2, nz)), dma((S, nz))] * 2
-        + [dma((4, S))] * 2,
+        + [dma((2 * S, 2, nz)), dma((2 * S, 2, nz)), dma((2 * S, 2, nz)), dma((2 * S, nz))]
+        + [dma((2, 2 * S))] * 2,
         compiler_params=pltpu.CompilerParams(
             collective_id=0, has_side_effects=True, vmem_limit_bytes=37 * 1024 * 1024
         ),

time: 145 us -> 160 us (1.10)
  Pallas kernels: 144 us -> 159 us
    pallas_call x1, Pallas kernels: 135 us -> 149 us  [per_device(): pl.pallas_call(functools.partial(layer_kernel, (nb, nz, S, H, K, W, slots...]
where the time goes in v4:
time: 160 us
  Pallas kernels  159 us (99%)
    pallas_call x1, Pallas kernels, per_device(): pl.pallas_call(functools.partial(layer_kernel, (nb, nz, S, H, K, W, slots...  149 us
    pallas_call x1, Pallas kernels, per_device(): pl.pallas_call(store_kernel, out_shape=(input_shape, input_shape, jax.Sha...  9.86 us

profile of v4, /device:TPU:0, one launch (start us, length us, event | category | flops | bytes accessed | tf_op | source)
XLA Modules:
  0.0 159.8 jit_solution(8152923393469300522)
XLA Ops:
  0.6 0.0 copy-start.3
  0.7 0.0 copy-start.2
  0.7 0.0 copy-start.1
  0.7 0.0 copy-start
  0.7 149.2 %shard_map.222 = (bf16[8,32,192,128]{3,2,1,0:T(8,128)(2,1)S(1)}, bf16[8,32,192,128]{3,2,1,0:T(8,128)(2,1)S(1)}, f32[8,48,384]{2,1,0:T(8,128)S(1)}, f32[48,192]{1...) custom-call(bf16[8,32,192,128]{3,2,1,0:T(8,128)(2,1)} %x_hbm.1, bf16[8,32,192,128]{3,2,1,0:T(8,128)(2,1)} %ct_hbm.1, ...), custom_call_target="tpu_custom_call" | custom-call | tf_op jit(solution)/shard_map/pallas_call | solution.py:680
  149.9 0.0 copy-done.3
  149.9 0.0 copy-done.2
  149.9 0.0 copy-done.1
  149.9 0.0 copy-done
  149.9 9.9 %shard_map.223 = (bf16[8,32,192,128]{3,2,1,0:T(8,128)(2,1)}, bf16[8,32,192,128]{3,2,1,0:T(8,128)(2,1)}, f32[8,48,384]{2,1,0:T(8,128)}, f32[8,48,384]{2,1,0:T(8,1...) custom-call(bf16[8,32,192,128]{3,2,1,0:T(8,128)(2,1)S(1)} %get-tuple, ...), custom_call_target="tpu_custom_call" | custom-call | tf_op jit(solution)/shard_map/pallas_call | solution.py:732
Async XLA Ops:
  0.6 149.2 %copy-start.3 = (f32[48,192]{1,0:T(8,128)S(1)}, f32[48,192]{1,0:T(8,128)}, u32[]{:S(2)}) copy-start(f32[48,192]{1,0:T(8,128)} %point_momentum_ref.3) | copy-start | bytes 110596
  0.7 149.2 %copy-start.2 = (f32[48,192]{1,0:T(8,128)S(1)}, f32[48,192]{1,0:T(8,128)}, u32[]{:S(2)}) copy-start(f32[48,192]{1,0:T(8,128)} %point_ref.3) | copy-start | bytes 110596
  0.7 149.2 %copy-start.1 = (f32[8,48,384]{2,1,0:T(8,128)S(1)}, f32[8,48,384]{2,1,0:T(8,128)}, u32[]{:S(2)}) copy-start(f32[8,48,384]{2,1,0:T(8,128)} %momentum_ref.1) | copy-start | bytes 1769476
  0.7 149.2 %copy-start = (f32[8,48,384]{2,1,0:T(8,128)S(1)}, f32[8,48,384]{2,1,0:T(8,128)}, u32[]{:S(2)}) copy-start(f32[8,48,384]{2,1,0:T(8,128)} %master_ref.1) | copy-start | bytes 1769476

commit v5 on v3

--- a/solution.py
+++ b/solution.py
@@ -139,60 +139,57 @@
         return carry
 
     lax.fori_loop(1, nz, greet_z, 0)
-    for one in loads:
-        one.start()
-
-    def load_x(s, carry):
-        x_copy(s).start()
-        return carry
-
-    def load_ct(s, carry):
-        ct_copy(s).start()
-        return carry
-
-    lax.fori_loop(0, S, load_x, 0)
-    lax.fori_loop(0, S, load_ct, 0)
-    ect_copy(0).start()
+    x_copy(0).start()
+    loads[1].start()
+    x_copy(1).start()
+    loads[0].start()
+    loads[2].start()
+    x_copy(2).start()
+    loads[3].start()
     cols[...] = jnp.zeros_like(cols)
     gk_ref[...] = jnp.zeros_like(gk_ref)
-    wm[...] = jnp.zeros_like(wm)
-
-    local = COLUMN_MODES // nz
-    lane = lax.broadcasted_iota(jnp.int32, (1, 2 * M), 1)
-
-    def place(d, carry):
-        for i in range(slots):
-            mode = owner_ref[(d * nz + z) * slots + i]
-            at = lax.div(mode, COLUMN_MODES) * local + lax.rem(mode, local)
-            lows[pl.ds(d * slots + i, 1), :] = jnp.where(lane == at, 1.0, 0.0)
-            highs[pl.ds(d * slots + i, 1), :] = jnp.where(lane == at + M, 1.0, 0.0)
-        return carry
-
-    lax.fori_loop(0, nb, place, 0)
-    inner = 1.0 / (H * nz * H * nz)
-    weigh = jnp.where(z * local + lax.rem(lane, local) == 0, 0.5 * inner, inner)
-    for table, pick in enumerate((lambda v: v[...], lambda v: v[...] * weigh)):
-        perm_ref[table] = pick(lows)[:, 0:M].astype(BF16)
-        back_ref[1 - table, 0] = pick(lows).astype(BF16)
-        back_ref[1 - table, 1] = pick(highs).astype(BF16)
-
-    weight = point_ref[...].astype(BF16)
-    kernel_t = jnp.concatenate([dot(weight, sign_ref[k]) for k in range(4)], axis=0)
-    kt1[...] = kernel_t[:, 0:128].astype(BF16)
-    for turn in range(8):
-        ktb[turn] = pltpu.roll(kernel_t[:, 128:256], (64 + 16 * turn) % 128, 1)
-    padded = jnp.concatenate([kernel_t.astype(BF16), jnp.zeros((256 - K, 256), BF16)], axis=0)
-    kernel_n = dot_nt(eye_ref[0:K], padded)
-    kk1[...] = kernel_n[:, 0:128].astype(BF16)
-    for turn in range(8):
-        kkb[turn] = pltpu.roll(kernel_n[:, 128:256], (64 + 16 * turn) % 128, 1)
-    for one in loads:
-        one.wait()
-    masters = master_ref[...].reshape(slots * channels, wide).astype(BF16)
-    for part in range(4):
-        block = dot(masters, psi[part]).astype(BF16)
-        for i in range(slots):
-            wm[i, part * channels : (part + 1) * channels, :] = block[i * channels : (i + 1) * channels]
+
+    def place_modes():
+        local = COLUMN_MODES // nz
+        lane = lax.broadcasted_iota(jnp.int32, (1, 2 * M), 1)
+
+        def place(d, carry):
+            for i in range(slots):
+                mode = owner_ref[(d * nz + z) * slots + i]
+                at = lax.div(mode, COLUMN_MODES) * local + lax.rem(mode, local)
+                lows[pl.ds(d * slots + i, 1), :] = jnp.where(lane == at, 1.0, 0.0)
+                highs[pl.ds(d * slots + i, 1), :] = jnp.where(lane == at + M, 1.0, 0.0)
+            return carry
+
+        lax.fori_loop(0, nb, place, 0)
+        inner = 1.0 / (H * nz * H * nz)
+        weigh = jnp.where(z * local + lax.rem(lane, local) == 0, 0.5 * inner, inner)
+        for table, pick in enumerate((lambda v: v[...], lambda v: v[...] * weigh)):
+            perm_ref[table] = pick(lows)[:, 0:M].astype(BF16)
+            back_ref[1 - table, 0] = pick(lows).astype(BF16)
+            back_ref[1 - table, 1] = pick(highs).astype(BF16)
+
+    def point_kernels():
+        weight = point_ref[...].astype(BF16)
+        kernel_t = jnp.concatenate([dot(weight, sign_ref[k]) for k in range(4)], axis=0)
+        kt1[...] = kernel_t[:, 0:128].astype(BF16)
+        for turn in range(8):
+            ktb[turn] = pltpu.roll(kernel_t[:, 128:256], (64 + 16 * turn) % 128, 1)
+        padded = jnp.concatenate([kernel_t.astype(BF16), jnp.zeros((256 - K, 256), BF16)], axis=0)
+        kernel_n = dot_nt(eye_ref[0:K], padded)
+        kk1[...] = kernel_n[:, 0:128].astype(BF16)
+        for turn in range(8):
+            kkb[turn] = pltpu.roll(kernel_n[:, 128:256], (64 + 16 * turn) % 128, 1)
+
+    def expand_weights():
+        loads[0].wait()
+        loads[2].wait()
+        wm[...] = jnp.zeros_like(wm)
+        masters = master_ref[...].reshape(slots * channels, wide).astype(BF16)
+        for part in range(4):
+            block = dot(masters, psi[part]).astype(BF16)
+            for i in range(slots):
+                wm[i, part * channels : (part + 1) * channels, :] = block[i * channels : (i + 1) * channels]
 
     def rs_copy(s, up, c, pb, rb, ssem, rsem):
         way = 0 if up else 1
@@ -524,6 +521,7 @@
         lax.fori_loop(1, nz, send, 0)
 
     def slot_gradients():
+        loads[3].wait()
         for i in range(slots):
             g_all = jnp.concatenate([by_column(gr, s, i) for s in range(S)], axis=0)
             x_all = jnp.concatenate([by_column(xr, s, i) for s in range(S)], axis=0)
@@ -594,7 +592,7 @@
         (16, stage_e),
     ]
     steps = S + max(lag for lag, _ in schedule)
-    at_step = {S + 8: point_first, S + 9: point_second, S + 11: point_update, S + 12: slot_gradients}
+    at_step = {0: place_modes, 1: expand_weights, 2: point_kernels, S + 8: point_first, S + 9: point_second, S + 11: point_update, S + 12: slot_gradients}
     groups = [range(slots)[: slots // 2], range(slots)[slots // 2 :]]
     for step, group in enumerate(groups):
         if group:
@@ -602,7 +600,12 @@
 
     pl.semaphore_wait(barrier, nb + nz - 2)
 
+    loads[1].wait()
+
     def iteration(t, carry):
+        pl.when(t + 3 < S)(lambda: x_copy(t + 3).start())
+        pl.when((t >= 5) & (t < S + 5))(lambda: ct_copy(t - 5).start())
+        pl.when(t == 14)(lambda: ect_copy(0).start())
         for lag, stage in schedule:
             s = t - lag
             pl.when((s >= 0) & (s < S))(functools.partial(stage, s))

time: 145 us -> 146 us (level)
  no operation moved by 1% of the time
where the time goes in v5:
time: 146 us
  Pallas kernels  145 us (99%)
    pallas_call x1, Pallas kernels, per_device(): pl.pallas_call(functools.partial(layer_kernel, (nb, nz, S, H, K, W, slots...  135 us
    pallas_call x1, Pallas kernels, per_device(): pl.pallas_call(store_kernel, out_shape=(input_shape, input_shape, jax.Sha...  9.86 us

profile of v5, /device:TPU:0, one launch (start us, length us, event | category | flops | bytes accessed | tf_op | source)
XLA Modules:
  0.0 145.5 jit_solution(6031564217673511360)
XLA Ops:
  0.6 0.0 copy-start.3
  0.7 0.0 copy-start.2
  0.7 0.0 copy-start.1
  0.7 0.0 copy-start
  0.7 134.9 %shard_map.222 = (bf16[8,32,192,128]{3,2,1,0:T(8,128)(2,1)S(1)}, bf16[8,32,192,128]{3,2,1,0:T(8,128)(2,1)S(1)}, f32[8,48,384]{2,1,0:T(8,128)S(1)}, f32[48,192]{1...) custom-call(bf16[8,32,192,128]{3,2,1,0:T(8,128)(2,1)} %x_hbm.1, bf16[8,32,192,128]{3,2,1,0:T(8,128)(2,1)} %ct_hbm.1, ...), custom_call_target="tpu_custom_call" | custom-call | tf_op jit(solution)/shard_map/pallas_call | solution.py:690
  135.6 0.0 copy-done.3
  135.6 0.0 copy-done.2
  135.7 0.0 copy-done.1
  135.7 0.0 copy-done
  135.7 9.9 %shard_map.223 = (bf16[8,32,192,128]{3,2,1,0:T(8,128)(2,1)}, bf16[8,32,192,128]{3,2,1,0:T(8,128)(2,1)}, f32[8,48,384]{2,1,0:T(8,128)}, f32[8,48,384]{2,1,0:T(8,1...) custom-call(bf16[8,32,192,128]{3,2,1,0:T(8,128)(2,1)S(1)} %get-tuple, ...), custom_call_target="tpu_custom_call" | custom-call | tf_op jit(solution)/shard_map/pallas_call | solution.py:746
Async XLA Ops:
  0.6 135.0 %copy-start.3 = (f32[48,192]{1,0:T(8,128)S(1)}, f32[48,192]{1,0:T(8,128)}, u32[]{:S(2)}) copy-start(f32[48,192]{1,0:T(8,128)} %point_momentum_ref.3) | copy-start | bytes 110596
  0.7 135.0 %copy-start.2 = (f32[48,192]{1,0:T(8,128)S(1)}, f32[48,192]{1,0:T(8,128)}, u32[]{:S(2)}) copy-start(f32[48,192]{1,0:T(8,128)} %point_ref.3) | copy-start | bytes 110596
  0.7 135.0 %copy-start.1 = (f32[8,48,384]{2,1,0:T(8,128)S(1)}, f32[8,48,384]{2,1,0:T(8,128)}, u32[]{:S(2)}) copy-start(f32[8,48,384]{2,1,0:T(8,128)} %momentum_ref.1) | copy-start | bytes 1769476
  0.7 135.0 %copy-start = (f32[8,48,384]{2,1,0:T(8,128)S(1)}, f32[8,48,384]{2,1,0:T(8,128)}, u32[]{:S(2)}) copy-start(f32[8,48,384]{2,1,0:T(8,128)} %master_ref.1) | copy-start | bytes 1769476

commit v6 on v5

--- a/solution.py
+++ b/solution.py
@@ -191,10 +191,13 @@
             for i in range(slots):
                 wm[i, part * channels : (part + 1) * channels, :] = block[i * channels : (i + 1) * channels]
 
-    def rs_copy(s, up, c, pb, rb, ssem, rsem):
+    pieces = 4
+
+    def rs_copy(s, up, c, pb, rb, ssem, rsem, piece=None):
         way = 0 if up else 1
+        rows = slice(None) if piece is None else pl.ds(piece * (M // pieces), M // pieces)
         return pltpu.make_async_remote_copy(
-            src_ref=pb.at[s, c], dst_ref=rb.at[s, way, c],
+            src_ref=pb.at[s, c, rows], dst_ref=rb.at[s, way, c, rows],
             send_sem=ssem.at[s, way, c], recv_sem=rsem.at[s, way, c],
             device_id=(me, z + 1 if up else z - 1), device_id_type=MESH,
         )
@@ -217,7 +220,8 @@
                         copy.wait_recv()
                         pb[s, c] = (pb[s, c].astype(F32) + rb[s, way, c].astype(F32)).astype(BF16)
 
-                    copy.start()
+                    for piece in range(pieces):
+                        rs_copy(s, up, c, *bufs, piece).start()
 
     def rs_final(s, bufs):
         pb, rb = bufs[0], bufs[1]
@@ -235,10 +239,11 @@
 
         return acc[...].astype(BF16)
 
-    def ag_copy(s, up, c, gb, ssem, rsem):
+    def ag_copy(s, up, c, gb, ssem, rsem, piece=None):
         way = 0 if up else 1
+        rows = slice(None) if piece is None else pl.ds(piece * (K // pieces), K // pieces)
         return pltpu.make_async_remote_copy(
-            src_ref=gb.at[s, c], dst_ref=gb.at[s, c],
+            src_ref=gb.at[s, c, rows], dst_ref=gb.at[s, c, rows],
             send_sem=ssem.at[s, way, c], recv_sem=rsem.at[s, c],
             device_id=(me, z + 1 if up else z - 1), device_id_type=MESH,
         )
@@ -260,7 +265,8 @@
                         if finish:
                             copy.wait_send()
                         else:
-                            copy.start()
+                            for piece in range(pieces):
+                                ag_copy(s, up, c, *bufs, piece).start()
 
     tiled = slots % 8 == 0
 

time: 146 us -> 147 us (level)
    pallas_call x1, Pallas kernels: 135 us -> 136 us  [per_device(): pl.pallas_call(functools.partial(layer_kernel, (nb, nz, S, H, K, W, slots...]
where the time goes in v6:
time: 147 us
  Pallas kernels  146 us (99%)
    pallas_call x1, Pallas kernels, per_device(): pl.pallas_call(functools.partial(layer_kernel, (nb, nz, S, H, K, W, slots...  136 us
    pallas_call x1, Pallas kernels, per_device(): pl.pallas_call(store_kernel, out_shape=(input_shape, input_shape, jax.Sha...  9.86 us

profile of v6, /device:TPU:0, one launch (start us, length us, event | category | flops | bytes accessed | tf_op | source)
XLA Modules:
  0.0 147.1 jit_solution(11005749540336362238)
XLA Ops:
  0.6 0.0 copy-start.3
  0.7 0.0 copy-start.2
  0.7 0.0 copy-start.1
  0.7 0.0 copy-start
  0.7 136.5 %shard_map.222 = (bf16[8,32,192,128]{3,2,1,0:T(8,128)(2,1)S(1)}, bf16[8,32,192,128]{3,2,1,0:T(8,128)(2,1)S(1)}, f32[8,48,384]{2,1,0:T(8,128)S(1)}, f32[48,192]{1...) custom-call(bf16[8,32,192,128]{3,2,1,0:T(8,128)(2,1)} %x_hbm.1, bf16[8,32,192,128]{3,2,1,0:T(8,128)(2,1)} %ct_hbm.1, ...), custom_call_target="tpu_custom_call" | custom-call | tf_op jit(solution)/shard_map/pallas_call | solution.py:696
  137.2 0.0 copy-done.3
  137.2 0.0 copy-done.2
  137.2 0.0 copy-done.1
  137.2 0.0 copy-done
  137.2 9.9 %shard_map.223 = (bf16[8,32,192,128]{3,2,1,0:T(8,128)(2,1)}, bf16[8,32,192,128]{3,2,1,0:T(8,128)(2,1)}, f32[8,48,384]{2,1,0:T(8,128)}, f32[8,48,384]{2,1,0:T(8,1...) custom-call(bf16[8,32,192,128]{3,2,1,0:T(8,128)(2,1)S(1)} %get-tuple, ...), custom_call_target="tpu_custom_call" | custom-call | tf_op jit(solution)/shard_map/pallas_call | solution.py:752
Async XLA Ops:
  0.6 136.5 %copy-start.3 = (f32[48,192]{1,0:T(8,128)S(1)}, f32[48,192]{1,0:T(8,128)}, u32[]{:S(2)}) copy-start(f32[48,192]{1,0:T(8,128)} %point_momentum_ref.3) | copy-start | bytes 110596
  0.7 136.5 %copy-start.2 = (f32[48,192]{1,0:T(8,128)S(1)}, f32[48,192]{1,0:T(8,128)}, u32[]{:S(2)}) copy-start(f32[48,192]{1,0:T(8,128)} %point_ref.3) | copy-start | bytes 110596
  0.7 136.5 %copy-start.1 = (f32[8,48,384]{2,1,0:T(8,128)S(1)}, f32[8,48,384]{2,1,0:T(8,128)}, u32[]{:S(2)}) copy-start(f32[8,48,384]{2,1,0:T(8,128)} %momentum_ref.1) | copy-start | bytes 1769476
  0.7 136.5 %copy-start = (f32[8,48,384]{2,1,0:T(8,128)S(1)}, f32[8,48,384]{2,1,0:T(8,128)}, u32[]{:S(2)}) copy-start(f32[8,48,384]{2,1,0:T(8,128)} %master_ref.1) | copy-start | bytes 1769476

commit v7 on v5

--- a/solution.py
+++ b/solution.py
@@ -219,21 +219,19 @@
 
                     copy.start()
 
-    def rs_final(s, bufs):
+    def rs_final(s, bufs, e):
         pb, rb = bufs[0], bufs[1]
-        acc[...] = pb[s, z].astype(F32)
+        acc[e] = pb[s, z].astype(F32)
 
         @pl.when(z > 0)
         def _():
             rs_copy(s, True, z, *bufs).wait_recv()
-            acc[...] += rb[s, 0, z].astype(F32)
+            acc[e] += rb[s, 0, z].astype(F32)
 
         @pl.when(z < last)
         def _():
             rs_copy(s, False, z, *bufs).wait_recv()
-            acc[...] += rb[s, 1, z].astype(F32)
-
-        return acc[...].astype(BF16)
+            acc[e] += rb[s, 1, z].astype(F32)
 
     def ag_copy(s, up, c, gb, ssem, rsem):
         way = 0 if up else 1
@@ -264,57 +262,57 @@
 
     tiled = slots % 8 == 0
 
-    def block_of(ref, s, d):
+    def block_of(ref, h, d):
         if tiled:
-            return ref.at[s, :, pl.ds(pl.multiple_of(d * slots, slots), slots)]
-        return ref.at[s, d]
-
-    def blocks_of(ref, s):
+            return ref.at[h, :, :, pl.ds(pl.multiple_of(d * slots, slots), slots)]
+        return ref.at[h, :, d]
+
+    def blocks_of(ref, h):
         if tiled:
-            return ref.at[s, :, pl.ds(0, (nb - 1) * slots)]
-        return ref.at[s, pl.ds(0, nb - 1)]
-
-    def whole_of(ref, s):
+            return ref.at[h, :, :, pl.ds(0, (nb - 1) * slots)]
+        return ref.at[h, :, pl.ds(0, nb - 1)]
+
+    def whole_of(ref, h, e):
         if tiled:
-            return jnp.concatenate([ref[s, g] for g in range(wide // 128)], axis=1)
-        return ref[s].reshape(nb * slots, wide)
-
-    def put_whole(ref, s, value):
+            return jnp.concatenate([ref[h, e, g] for g in range(wide // 128)], axis=1)
+        return ref[h, e].reshape(nb * slots, wide)
+
+    def put_whole(ref, h, e, value):
         if tiled:
             for g in range(wide // 128):
-                ref[s, g] = value[:, g * 128 : (g + 1) * 128]
+                ref[h, e, g] = value[:, g * 128 : (g + 1) * 128]
         else:
-            ref[s] = value.reshape(nb, slots, wide)
-
-    def slot_rows(ref, s, i):
+            ref[h, e] = value.reshape(nb, slots, wide)
+
+    def slot_rows(ref, h, e, i):
         if tiled:
-            return jnp.concatenate([ref[s, g, pl.ds(i, nb, stride=slots), :] for g in range(wide // 128)], axis=1)
-        return ref[s, :, i, :]
-
-    def put_slot_rows(ref, s, i, value):
+            return jnp.concatenate([ref[h, e, g, pl.ds(i, nb, stride=slots), :] for g in range(wide // 128)], axis=1)
+        return ref[h, e, :, i, :]
+
+    def put_slot_rows(ref, h, e, i, value):
         if tiled:
             for g in range(wide // 128):
-                ref[s, g, pl.ds(i, nb, stride=slots), :] = value[:, g * 128 : (g + 1) * 128]
+                ref[h, e, g, pl.ds(i, nb, stride=slots), :] = value[:, g * 128 : (g + 1) * 128]
         else:
-            ref[s, :, i, :] = value
-
-    def exchange(s, src, dst, which):
+            ref[h, e, :, i, :] = value
+
+    def exchange(h, src, dst, which):
         def send(d, carry):
             peer = lax.rem(me + d, nb)
             pltpu.make_async_remote_copy(
-                src_ref=block_of(src, s, peer), dst_ref=block_of(dst, s, me),
-                send_sem=a2a_s.at[which, s], recv_sem=a2a_r.at[which, s],
+                src_ref=block_of(src, h, peer), dst_ref=block_of(dst, h, me),
+                send_sem=a2a_s.at[which, h], recv_sem=a2a_r.at[which, h],
                 device_id=(peer, z), device_id_type=MESH,
             ).start()
             return carry
 
         lax.fori_loop(1, nb, send, 0)
-        block_of(dst, s, me)[...] = block_of(src, s, me)[...]
-
-    def exchanged(s, src, dst, which):
+        block_of(dst, h, me)[...] = block_of(src, h, me)[...]
+
+    def exchanged(h, src, dst, which):
         return pltpu.make_async_remote_copy(
-            src_ref=blocks_of(src, s), dst_ref=blocks_of(dst, s),
-            send_sem=a2a_s.at[which, s], recv_sem=a2a_r.at[which, s],
+            src_ref=blocks_of(src, h), dst_ref=blocks_of(dst, h),
+            send_sem=a2a_s.at[which, h], recv_sem=a2a_r.at[which, h],
             device_id=(lax.rem(me + 1, nb), z), device_id_type=MESH,
         )
 
@@ -349,50 +347,65 @@
         forward_rows(s, pb1)
         rs_hop(0, s, rs1)
 
-    def by_column(ref, s, i):
-        rows = slot_rows(ref, s, i)
-        low, mid, top = rows[:, 0:128], rows[:, 128:256], rows[:, 256:384]
-        first = jnp.concatenate([low, mid], axis=1)
-        second = jnp.concatenate([top, pltpu.roll(mid, 64, 1)], axis=1)
-        return jnp.concatenate([first, second], axis=0).astype(BF16)
-
-    def put_by_column(ref, s, i, value):
-        first, second = value[0:nb], value[nb:]
-        mid = first[:, 128:256] + pltpu.roll(second[:, 128:256], 64, 1)
-        put_slot_rows(ref, s, i, jnp.concatenate([first[:, 0:128], mid, second[:, 0:128]], axis=1))
+    def by_column(ref, h, i):
+        first, second = [], []
+        for e in range(2):
+            rows = slot_rows(ref, h, e, i)
+            low, mid, top = rows[:, 0:128], rows[:, 128:256], rows[:, 256:384]
+            first.append(jnp.concatenate([low, mid], axis=1))
+            second.append(jnp.concatenate([top, pltpu.roll(mid, 64, 1)], axis=1))
+        return jnp.concatenate(first + second, axis=0).astype(BF16)
+
+    def put_by_column(ref, h, i, value):
+        for e in range(2):
+            first, second = value[e * nb : (e + 1) * nb], value[(2 + e) * nb : (3 + e) * nb]
+            mid = first[:, 128:256] + pltpu.roll(second[:, 128:256], 64, 1)
+            put_slot_rows(ref, h, e, i, jnp.concatenate([first[:, 0:128], mid, second[:, 0:128]], axis=1))
 
     def stage_b(s):
-        exchanged(s, xs, xr, 0).wait_recv()
+        h = lax.div(s, 2)
+        exchanged(h, xs, xr, 0).wait_recv()
         for i in range(slots):
-            put_by_column(ps, s, i, dot_nt(by_column(xr, s, i), wm[i]))
-        exchange(s, ps, pr, 1)
+            put_by_column(ps, h, i, dot_nt(by_column(xr, h, i), wm[i]))
+        exchange(h, ps, pr, 1)
 
     def stage_d(s):
-        exchanged(s, gs, gr, 2).wait_recv()
+        h = lax.div(s, 2)
+        exchanged(h, gs, gr, 2).wait_recv()
         for i in range(slots):
-            put_by_column(hs, s, i, dot(by_column(gr, s, i), wm[i]))
-        exchange(s, hs, hr, 3)
+            put_by_column(hs, h, i, dot(by_column(gr, h, i), wm[i]))
+        exchange(h, hs, hr, 3)
 
     def stage_f(s, bufs, table, src, dst, which):
-        placed = dot(perm_ref[table], rs_final(s, bufs)).astype(BF16)
-        put_whole(src, s, dot(placed, turn_ref[...]))
-        exchange(s, src, dst, which)
+        h = lax.div(s, 2)
+        for e in range(2):
+            rs_final(s - 1 + e, bufs, e)
+        placed = [dot(perm_ref[table], acc[e].astype(BF16)).astype(BF16) for e in range(2)]
+        both = dot(jnp.concatenate(placed, axis=0), turn_ref[...])
+        for e in range(2):
+            put_whole(src, h, e, both[e * M : (e + 1) * M])
+        exchange(h, src, dst, which)
 
     def stage_u(s, bufs, table, src, dst, which):
-        exchanged(s, src, dst, which).wait_recv()
-        turned = jnp.transpose(whole_of(dst, s))
-        cut = K // 128 * 128
-        first = turned[0:K]
-        second = jnp.concatenate([turned[2 * K - cut :], turned[K : 2 * K - cut]], axis=0)
-        parts = []
-        for q in range(2):
-            base = 2 * q * channels
-            at = lambda col, row: col[base + row * channels : base + (row + 1) * channels]
-            m00, m10, m01, m11 = at(first, 0), at(first, 1), at(second, 0), at(second, 1)
-            parts.append(jnp.concatenate([m00 + m11, m00 - m11, m01 + m10, m01 - m10], axis=0).astype(BF16))
-        both = dot(parts[0], back_ref[table, 0]) + dot(parts[1], back_ref[table, 1])
-        bufs[0][s, z] = both.astype(BF16)
-        ag_hop(0, s, bufs)
+        h = lax.div(s, 2)
+        exchanged(h, src, dst, which).wait_recv()
+        for e in range(2):
+            turned = jnp.transpose(whole_of(dst, h, e))
+            cut = K // 128 * 128
+            first = turned[0:K]
+            second = jnp.concatenate([turned[2 * K - cut :], turned[K : 2 * K - cut]], axis=0)
+            parts = []
+            for q in range(2):
+                base = 2 * q * channels
+                at = lambda col, row: col[base + row * channels : base + (row + 1) * channels]
+                m00, m10, m01, m11 = at(first, 0), at(first, 1), at(second, 0), at(second, 1)
+                parts.append(jnp.concatenate([m00 + m11, m00 - m11, m01 + m10, m01 - m10], axis=0).astype(BF16))
+            bufs[0][s - 1 + e, z] = (dot(parts[0], back_ref[table, 0]) + dot(parts[1], back_ref[table, 1])).astype(BF16)
+        gather(0, s, bufs)
+
+    def gather(j, s, bufs):
+        for e in range(2):
+            ag_hop(j, s - 1 + e, bufs)
 
     def inverse_rows(s, gb, base):
         spread = dot(gb[s].reshape(nz * K, 2 * M), single[...])
@@ -523,8 +536,8 @@
     def slot_gradients():
         loads[3].wait()
         for i in range(slots):
-            g_all = jnp.concatenate([by_column(gr, s, i) for s in range(S)], axis=0)
-            x_all = jnp.concatenate([by_column(xr, s, i) for s in range(S)], axis=0)
+            g_all = jnp.concatenate([by_column(gr, h, i) for h in range(S // 2)], axis=0)
+            x_all = jnp.concatenate([by_column(xr, h, i) for h in range(S // 2)], axis=0)
             g_turned = dot_nt(eye_ref[...], g_all).astype(BF16)
             wm[i] = dot(g_turned, x_all).astype(BF16)
 
@@ -572,31 +585,37 @@
     ag1 = (gb1, ag1_s, ag1_r)
     ag2 = (gb2, ag2_s, ag2_r)
 
+    def odd(stage):
+        return lambda s: pl.when(lax.rem(s, 2) == 1)(functools.partial(stage, s))
+
     schedule = [
         (0, stage_a),
-        (3, lambda s: stage_f(s, rs1, 0, xs, xr, 0)),
-        (11, lambda s: stage_f(s, rs2, 1, gs, gr, 2)),
+        (3, odd(lambda s: stage_f(s, rs1, 0, xs, xr, 0))),
+        (12, odd(lambda s: stage_f(s, rs2, 1, gs, gr, 2))),
         (2, lambda s: rs_hop(2, s, rs1)),
-        (10, lambda s: rs_hop(2, s, rs2)),
+        (11, lambda s: rs_hop(2, s, rs2)),
         (1, lambda s: rs_hop(1, s, rs1)),
-        (9, lambda s: rs_hop(1, s, rs2)),
-        (7, lambda s: ag_hop(2, s, ag1)),
-        (15, lambda s: ag_hop(2, s, ag2)),
-        (6, lambda s: ag_hop(1, s, ag1)),
-        (14, lambda s: ag_hop(1, s, ag2)),
-        (5, lambda s: stage_u(s, ag1, 0, ps, pr, 1)),
-        (13, lambda s: stage_u(s, ag2, 1, hs, hr, 3)),
-        (4, stage_b),
-        (12, stage_d),
-        (8, stage_c),
-        (16, stage_e),
+        (10, lambda s: rs_hop(1, s, rs2)),
+        (7, odd(lambda s: gather(2, s, ag1))),
+        (16, odd(lambda s: gather(2, s, ag2))),
+        (6, odd(lambda s: gather(1, s, ag1))),
+        (15, odd(lambda s: gather(1, s, ag2))),
+        (5, odd(lambda s: stage_u(s, ag1, 0, ps, pr, 1))),
+        (14, odd(lambda s: stage_u(s, ag2, 1, hs, hr, 3))),
+        (4, odd(stage_b)),
+        (13, odd(stage_d)),
+        (9, stage_c),
+        (18, stage_e),
     ]
     steps = S + max(lag for lag, _ in schedule)
-    at_step = {0: place_modes, 1: expand_weights, 2: point_kernels, S + 8: point_first, S + 9: point_second, S + 11: point_update, S + 12: slot_gradients}
+    at_step = {
+        0: place_modes, 1: expand_weights, 2: point_kernels, S + 9: point_first, S + 10: point_second, S + 12: point_update,
+        S + 13: slot_gradients,
+    }
     groups = [range(slots)[: slots // 2], range(slots)[slots // 2 :]]
     for step, group in enumerate(groups):
         if group:
-            at_step[S + 13 + step] = functools.partial(slot_updates, group)
+            at_step[S + 14 + step] = functools.partial(slot_updates, group)
 
     pl.semaphore_wait(barrier, nb + nz - 2)
 
@@ -605,7 +624,7 @@
     def iteration(t, carry):
         pl.when(t + 3 < S)(lambda: x_copy(t + 3).start())
         pl.when((t >= 5) & (t < S + 5))(lambda: ct_copy(t - 5).start())
-        pl.when(t == 14)(lambda: ect_copy(0).start())
+        pl.when(t == 16)(lambda: ect_copy(0).start())
         for lag, stage in schedule:
             s = t - lag
             pl.when((s >= 0) & (s < S))(functools.partial(stage, s))
@@ -621,11 +640,15 @@
             rs_hop(j, s, rs2, True)
             ag_hop(j, s, ag1, True)
             ag_hop(j, s, ag2, True)
+        return carry
+
+    def finish_exchanges(h, carry):
         for which, (src, dst) in enumerate(((xs, xr), (ps, pr), (gs, gr), (hs, hr))):
-            exchanged(s, src, dst, which).wait_send()
+            exchanged(h, src, dst, which).wait_send()
         return carry
 
     lax.fori_loop(0, S, finish, 0)
+    lax.fori_loop(0, S // 2, finish_exchanges, 0)
     all_but_one(pa, nb, pa_s, pa_r, (lax.rem(me + 1, nb), z)).wait_send()
     all_but_one(pz, nz, pz_s, pz_r, (me, lax.rem(z + 1, nz))).wait_send()
 
@@ -680,7 +703,7 @@
     anywhere = pl.BlockSpec(memory_space=pltpu.HBM)
     smem = pl.BlockSpec(memory_space=pltpu.SMEM)
     vmem = pl.BlockSpec(memory_space=pltpu.VMEM)
-    exchange_shape = (S, wide // 128, nb * slots, 128) if slots % 8 == 0 else (S, nb, slots, wide)
+    exchange_shape = (S // 2, 2, wide // 128, nb * slots, 128) if slots % 8 == 0 else (S // 2, 2, nb, slots, wide)
     dma = pltpu.SemaphoreType.DMA
     single = jnp.asarray(row_blocks(grid, nz))
     psi, turn, signs = (jnp.asarray(one) for one in product_signs(channels))
@@ -712,7 +735,7 @@
             pltpu.VMEM((8, K, 128), F32),
             pltpu.VMEM((K, 128), BF16),
             pltpu.VMEM((8, K, 128), F32),
-            pltpu.VMEM((M, wide), F32),
+            pltpu.VMEM((2, M, wide), F32),
             pltpu.VMEM((K, K), F32),
             pltpu.VMEM((nb, channels, K), F32),
             pltpu.VMEM((nz, channels, K), F32),
@@ -732,7 +755,7 @@
         + [dma((1,))] * 4
         + [dma((S, 2, nz))] * 4
         + [dma((S, 2, nz)), dma((S, nz))] * 2
-        + [dma((4, S))] * 2,
+        + [dma((4, S // 2))] * 2,
         compiler_params=pltpu.CompilerParams(
             collective_id=0, has_side_effects=True, vmem_limit_bytes=37 * 1024 * 1024
         ),

time: 146 us -> 153 us (1.048)
  Pallas kernels: 145 us -> 152 us
    pallas_call x1, Pallas kernels: 135 us -> 142 us  [per_device(): pl.pallas_call(functools.partial(layer_kernel, (nb, nz, S, H, K, W, slots...]
where the time goes in v7:
time: 153 us; the launch traced here: 152 us
  Pallas kernels  152 us (99%)
    pallas_call x1, Pallas kernels, per_device(): pl.pallas_call(functools.partial(layer_kernel, (nb, nz, S, H, K, W, slots...  142 us
    pallas_call x1, Pallas kernels, per_device(): pl.pallas_call(store_kernel, out_shape=(input_shape, input_shape, jax.Sha...  9.86 us

profile of v7, /device:TPU:0, one launch (start us, length us, event | category | flops | bytes accessed | tf_op | source)
XLA Modules:
  0.0 152.4 jit_solution(2043612648824481141)
XLA Ops:
  0.6 0.0 copy-start.3
  0.7 0.0 copy-start.2
  0.7 0.0 copy-start.1
  0.7 0.0 copy-start
  0.7 141.8 %shard_map.222 = (bf16[8,32,192,128]{3,2,1,0:T(8,128)(2,1)S(1)}, bf16[8,32,192,128]{3,2,1,0:T(8,128)(2,1)S(1)}, f32[8,48,384]{2,1,0:T(8,128)S(1)}, f32[48,192]{1...) custom-call(bf16[8,32,192,128]{3,2,1,0:T(8,128)(2,1)} %x_hbm.1, bf16[8,32,192,128]{3,2,1,0:T(8,128)(2,1)} %ct_hbm.1, ...), custom_call_target="tpu_custom_call" | custom-call | tf_op jit(solution)/shard_map/pallas_call | solution.py:713
  142.5 0.0 copy-done.3
  142.5 0.0 copy-done.2
  142.5 0.0 copy-done.1
  142.5 0.0 copy-done
  142.5 9.9 %shard_map.223 = (bf16[8,32,192,128]{3,2,1,0:T(8,128)(2,1)}, bf16[8,32,192,128]{3,2,1,0:T(8,128)(2,1)}, f32[8,48,384]{2,1,0:T(8,128)}, f32[8,48,384]{2,1,0:T(8,1...) custom-call(bf16[8,32,192,128]{3,2,1,0:T(8,128)(2,1)S(1)} %get-tuple, ...), custom_call_target="tpu_custom_call" | custom-call | tf_op jit(solution)/shard_map/pallas_call | solution.py:769
Async XLA Ops:
  0.6 141.8 %copy-start.3 = (f32[48,192]{1,0:T(8,128)S(1)}, f32[48,192]{1,0:T(8,128)}, u32[]{:S(2)}) copy-start(f32[48,192]{1,0:T(8,128)} %point_momentum_ref.3) | copy-start | bytes 110596
  0.7 141.8 %copy-start.2 = (f32[48,192]{1,0:T(8,128)S(1)}, f32[48,192]{1,0:T(8,128)}, u32[]{:S(2)}) copy-start(f32[48,192]{1,0:T(8,128)} %point_ref.3) | copy-start | bytes 110596
  0.7 141.8 %copy-start.1 = (f32[8,48,384]{2,1,0:T(8,128)S(1)}, f32[8,48,384]{2,1,0:T(8,128)}, u32[]{:S(2)}) copy-start(f32[8,48,384]{2,1,0:T(8,128)} %momentum_ref.1) | copy-start | bytes 1769476
  0.7 141.8 %copy-start = (f32[8,48,384]{2,1,0:T(8,128)S(1)}, f32[8,48,384]{2,1,0:T(8,128)}, u32[]{:S(2)}) copy-start(f32[8,48,384]{2,1,0:T(8,128)} %master_ref.1) | copy-start | bytes 1769476
